TPU v7x, 32 devices: a whole 2x2x4 slice. The times are simulated.
32 devices in a mesh: seq: 16 (over z, y, x), tp: 2 (over core).
Axes of the slice: x: 2, y: 2, z: 4, core: 2. Of those that a mesh axis runs over, the one named last changes fastest.
Arguments:
- cache_keys: bfloat16 [32768, 2048], P('seq', 'tp'), may hold values from -13 to 13
- cache_values: bfloat16 [32768, 2048], P('seq', 'tp'), may hold values from -12 to 12
- keep_flags: int32 [32768], P('seq'), may hold values from 0 to 1, as said below
- drop_weight: int32 [32768], P('seq'), may hold values from 1 to 255
- req_blocks: int32 [12], replicated, may hold values from 1 to 32, 256 in all
- queries: bfloat16 [12, 2048], P(None, 'tp'), may hold values from -48 to 48
- new_keys: bfloat16 [12, 2048], P(None, 'tp'), may hold values from -12 to 12
- new_values: bfloat16 [12, 2048], P(None, 'tp'), may hold values from -12 to 12
- out_weight: bfloat16 [2048, 2048], P('tp', 'seq'), may hold values from -0.125 to 0.125
Outputs:
- packed_keys: bfloat16 [16640, 2048], P('seq', 'tp')
- packed_values: bfloat16 [16640, 2048], P('seq', 'tp')
- packed_bias: bfloat16 [16640], P('seq')
- packed_request: int32 [16640], P('seq')
- layer_output: bfloat16 [12, 2048], P('tp', 'seq')
Inputs may be any that keep to these rules, and one draw needn't show every extreme that they name: `keep_flags`: every aligned block of 128 rows keeps between 32 and 64 rows; in every draw all blocks of the rows of some one index of seq keep exactly 64. `req_blocks`: the entries sum to 256; the largest is 32.
All inputs are finite; a program needn't handle non-finite values.
Results may differ from a plain program's by a relative error of at most 0.009.
Values may be sent and summed in bfloat16 or wider, within the bound.
No kernel may reach another device: no remote copies, remote signals or barrier semaphores. Data moves between devices by JAX's collectives and lax.ppermute only.
A program may use at most 64 MiB of HBM per device.

v0:
```python
import functools

import jax
import jax.numpy as jnp
from jax import lax
from jax.experimental import pallas as pl
from jax.experimental.pallas import tpu as pltpu
from jax.sharding import PartitionSpec as P

HD = 256
BLOCK = 128
LANES = 128
SUB = 16
LEAST_KEPT = BLOCK // 4
MOST_KEPT = BLOCK // 2
LOW = -1e30
VMEM_LIMIT = 56 * 1024 * 1024


class Geometry:
    def __init__(self, peers, blocks, features):
        self.peers = peers
        self.blocks = blocks
        self.features = features
        self.heads = features // HD
        self.slots = blocks * (MOST_KEPT + 1)
        self.peer_rows = -(-self.slots // peers)
        self.groups = self.peer_rows // SUB
        self.main = self.groups * SUB
        self.chunks = 2 * features // LANES
        self.tail = -(-self.chunks // SUB) * SUB
        self.slab = self.chunks * self.main + self.tail
        self.group_rows = SUB * peers
        assert self.peer_rows == self.main + 1
        self.join = min(peers, max(1, 256 // self.main))
        self.joins = peers // self.join
        window = self.join * self.peer_rows + SUB - 1
        self.window = min(-(-window // SUB) * SUB, self.slots)
        assert self.slots % SUB == 0 and peers % self.join == 0

    def block_range(self, first, last):
        low = max(0, -(-(first - MOST_KEPT) // (MOST_KEPT + 1)))
        high = min(self.blocks - 1, last // (LEAST_KEPT + 1))
        return low, high + 1


def iota(shape, axis):
    return lax.broadcasted_iota(jnp.int32, shape, axis)


def dot(a, b, contract=((1,), (0,))):
    return lax.dot_general(a, b, (contract, ((), ())), preferred_element_type=jnp.float32)


def pack_kernel(
    geo, keep_ref, weight_ref, first_ref, last_ref, query_ref, key_ref, value_ref,
    packed_ref, part_ref, pick_ref, scale_ref, fold_ref, left_ref,
):
    step = pl.program_id(0)
    blocks, peers = geo.blocks, geo.peers
    ranges = [
        geo.block_range(g * geo.group_rows, (g + 1) * geo.group_rows - 1) for g in range(geo.groups)
    ]
    places = []
    place = 0
    for low, high in ranges:
        places.append(place)
        place += (high - low) * BLOCK
    tail_low, tail_high = geo.block_range(geo.main * peers, geo.slots - 1)
    tail_place = place

    keep = keep_ref[...].astype(jnp.float32)
    kept = jnp.sum(keep, axis=1, keepdims=True)
    dropped = weight_ref[...].astype(jnp.float32) * (1.0 - keep)
    inverse = 1.0 / jnp.sum(dropped, axis=1, keepdims=True)

    @pl.when(step == 0)
    def _():
        earlier = (iota((BLOCK, BLOCK), 0) < iota((BLOCK, BLOCK), 1)).astype(jnp.bfloat16)
        within = dot(keep.astype(jnp.bfloat16), earlier)
        before = (iota((blocks, blocks), 1) < iota((blocks, blocks), 0)).astype(jnp.bfloat16)
        sizes = jnp.broadcast_to(kept + 1.0, (blocks, BLOCK)).astype(jnp.bfloat16)
        base = dot(before, sizes)
        entry = jnp.where(keep > 0.0, base + within, -1.0).astype(jnp.int32)
        fold_entry = (base + kept).astype(jnp.int32)

        def select(index, low, high, rows, place):
            scale = jnp.ones((rows, BLOCK), jnp.float32)
            for b in range(low, high):
                folds = index == fold_entry[b : b + 1, :]
                one = jnp.where(index == entry[b : b + 1, :], 1.0, 0.0)
                picked = jnp.where(folds, dropped[b : b + 1, :], one)
                at = place + (b - low) * BLOCK
                pick_ref[0:rows, at : at + BLOCK] = picked.astype(jnp.bfloat16)
                scale = jnp.where(folds, inverse[b : b + 1, :], scale)
            return scale

        rows = geo.group_rows
        row, col = iota((rows, BLOCK), 0), 0
        for g in range(geo.groups):
            index = (g * SUB + row % SUB) * peers + row // SUB
            scale_ref[g, :, :] = select(index, *ranges[g], rows, places[g])
        index = geo.main * peers + iota((peers, BLOCK), 0)
        scale_ref[geo.groups, 0:peers, :] = select(index, tail_low, tail_high, peers, tail_place)
        for b in range(blocks):
            mine = iota((blocks, BLOCK), 0) == b
            fold_ref[:, b * BLOCK : (b + 1) * BLOCK] = jnp.where(
                mine, dropped[b : b + 1, :], 0.0
            ).astype(jnp.bfloat16)

    for part, source in enumerate((key_ref, value_ref)):
        for g in range(geo.groups):
            low, high = ranges[g]
            rows = dot(
                pick_ref[:, places[g] : places[g] + (high - low) * BLOCK],
                source[low * BLOCK : high * BLOCK, :],
            )
            for half in range(HD // LANES):
                chunk = rows[:, half * LANES : (half + 1) * LANES] * scale_ref[g]
                chunk = chunk.astype(jnp.bfloat16).reshape(peers, SUB, LANES)
                at = pl.multiple_of(
                    (step * 4 + part * 2 + half) * geo.main + g * SUB, SUB
                )
                packed_ref[:, pl.ds(at, SUB), :] = chunk
        tail = dot(
            pick_ref[0:peers, tail_place : tail_place + (tail_high - tail_low) * BLOCK],
            source[tail_low * BLOCK : tail_high * BLOCK, :],
        )
        for half in range(HD // LANES):
            chunk = tail[:, half * LANES : (half + 1) * LANES] * scale_ref[geo.groups, 0:peers, :]
            at = pl.multiple_of((step * 4 + part * 2 + half) * peers, SUB)
            left_ref[pl.ds(at, peers), :] = chunk.astype(jnp.bfloat16)

    @pl.when(step == geo.heads - 1)
    def _():
        shape = (peers * geo.tail, geo.chunks * peers)
        row, col = iota(shape, 0), iota(shape, 1)
        wanted = row % geo.tail * peers + row // geo.tail
        turn = jnp.where(wanted == col, 1.0, 0.0).astype(jnp.bfloat16)
        tails = dot(turn, left_ref[...]).astype(jnp.bfloat16).reshape(peers, geo.tail, LANES)
        packed_ref[:, geo.chunks * geo.main :, :] = tails

    query = query_ref[...]
    first, last = first_ref[...], last_ref[...]
    requests = query.shape[0]
    score_scale = HD**-0.5
    folded_keys = (dot(fold_ref[...], key_ref[...]) * inverse).astype(jnp.bfloat16)
    folded_values = (dot(fold_ref[...], value_ref[...]) * inverse).astype(jnp.bfloat16)
    ones = jnp.ones((8, BLOCK), jnp.bfloat16)
    kept_lanes = dot(ones, keep.astype(jnp.bfloat16), ((1,), (1,)))[0:1, :]
    bias = jnp.log(BLOCK - kept_lanes).astype(jnp.bfloat16).astype(jnp.float32)
    fold_scores = dot(query, folded_keys, ((1,), (1,))) * score_scale + bias
    block = iota((requests, blocks), 1)
    fold_member = (block >= first) & (block < last)
    fold_scores = jnp.where(fold_member, fold_scores, LOW)
    scores = dot(query, key_ref[...], ((1,), (1,))) * score_scale
    lane_block = iota((requests, blocks * BLOCK), 1) // BLOCK
    kept_rows = jnp.concatenate(
        [jnp.broadcast_to(keep[b : b + 1, :], (requests, BLOCK)) for b in range(blocks)], axis=1
    )
    member = (lane_block >= first) & (lane_block < last) & (kept_rows > 0.0)
    scores = jnp.where(member, scores, LOW)
    peak = jnp.maximum(
        jnp.max(scores, axis=1, keepdims=True), jnp.max(fold_scores, axis=1, keepdims=True)
    )
    probs = jnp.where(member, jnp.exp(scores - peak), 0.0)
    fold_probs = jnp.where(fold_member, jnp.exp(fold_scores - peak), 0.0)
    total = jnp.sum(probs, axis=1, keepdims=True) + jnp.sum(fold_probs, axis=1, keepdims=True)
    mixed = dot(probs.astype(jnp.bfloat16), value_ref[...]) + dot(
        fold_probs.astype(jnp.bfloat16), folded_values
    )
    part_ref[0, :, 0:HD] = mixed
    part_ref[0, :, HD:] = jnp.where(iota((requests, LANES), 1) < LANES // 2, peak, total)


def pack(geo, keep, weight, first, last, queries, cache_keys, cache_values):
    rows = cache_keys.shape[0]
    requests = queries.shape[0]
    width = 0
    for g in range(geo.groups):
        low, high = geo.block_range(g * geo.group_rows, (g + 1) * geo.group_rows - 1)
        width += (high - low) * BLOCK
    low, high = geo.block_range(geo.main * geo.peers, geo.slots - 1)
    width += (high - low) * BLOCK
    whole = lambda *shape: pl.BlockSpec(shape, lambda t: (0,) * len(shape))
    return pl.pallas_call(
        functools.partial(pack_kernel, geo),
        grid=(geo.heads,),
        in_specs=[
            whole(geo.blocks, BLOCK),
            whole(geo.blocks, BLOCK),
            whole(requests, 1),
            whole(requests, 1),
            pl.BlockSpec((requests, HD), lambda t: (0, t)),
            pl.BlockSpec((rows, HD), lambda t: (0, t)),
            pl.BlockSpec((rows, HD), lambda t: (0, t)),
        ],
        out_specs=[
            whole(geo.peers, geo.slab, LANES),
            pl.BlockSpec((1, requests, HD + LANES), lambda t: (t, 0, 0)),
        ],
        out_shape=[
            jax.ShapeDtypeStruct((geo.peers, geo.slab, LANES), jnp.bfloat16),
            jax.ShapeDtypeStruct((geo.heads, requests, HD + LANES), jnp.float32),
        ],
        scratch_shapes=[
            pltpu.VMEM((geo.group_rows, width), jnp.bfloat16),
            pltpu.VMEM((geo.groups + 1, geo.group_rows, BLOCK), jnp.float32),
            pltpu.VMEM((geo.blocks, rows), jnp.bfloat16),
            pltpu.VMEM((geo.chunks * geo.peers, LANES), jnp.bfloat16),
        ],
        compiler_params=pltpu.CompilerParams(vmem_limit_bytes=VMEM_LIMIT),
        cost_estimate=pl.CostEstimate(
            flops=2 * geo.group_rows * width * 2 * geo.features,
            bytes_accessed=3 * rows * geo.features * 2,
            transcendentals=0,
        ),
    )(keep, weight, first, last, queries, cache_keys, cache_values)


def turn_kernel(geo, start_ref, packed_ref, sent_ref, sems):
    start = start_ref[0]
    copies = []
    for d in range(geo.peers):
        group = lax.rem(d + geo.peers - start, geo.peers)
        copies.append(pltpu.make_async_copy(packed_ref.at[group], sent_ref.at[d], sems.at[d]))
    for copy in copies:
        copy.start()
    for copy in copies:
        copy.wait()


def turn(geo, start, packed):
    return pl.pallas_call(
        functools.partial(turn_kernel, geo),
        in_specs=[pl.BlockSpec(memory_space=pltpu.SMEM), pl.BlockSpec(memory_space=pl.ANY)],
        out_specs=pl.BlockSpec(memory_space=pl.ANY),
        out_shape=jax.ShapeDtypeStruct(packed.shape, packed.dtype),
        scratch_shapes=[pltpu.SemaphoreType.DMA((geo.peers,))],
        cost_estimate=pl.CostEstimate(flops=0, bytes_accessed=2 * packed.size * 2, transcendentals=0),
    )(start, packed)


def unpack_kernel(geo, slot_ref, slab_ref, tail_ref, keys_ref, values_ref, pick_ref, tails_ref):
    step = pl.program_id(0)
    peers, main = geo.peers, geo.main
    width = geo.join * main
    lows = []
    for q in range(geo.joins):
        low = jnp.minimum(slot_ref[q * geo.join] // SUB * SUB, geo.slots - geo.window)
        lows.append(pl.multiple_of(low, SUB))

    @pl.when(step == 0)
    def _():
        for q in range(geo.joins):
            lane = iota((1, width), 1)
            target = lane % main
            last = iota((1, peers), 1) * 0 - 1
            for j in range(geo.join):
                at = slot_ref[q * geo.join + j] - lows[q]
                target = target + jnp.where(lane // main == j, at, 0)
                last = jnp.where(iota((1, peers), 1) == q * geo.join + j, at + main, last)
            picked = jnp.where(iota((geo.window, width), 0) == target, 1.0, 0.0)
            pick_ref[q, :, 0:width] = picked.astype(jnp.bfloat16)
            picked = jnp.where(iota((geo.window, peers), 0) == last, 1.0, 0.0)
            pick_ref[q, :, width : width + peers] = picked.astype(jnp.bfloat16)
        shape = (geo.chunks * peers, peers * geo.tail)
        row, col = iota(shape, 0), iota(shape, 1)
        wanted = row % peers * geo.tail + row // peers
        back = jnp.where(wanted == col, 1.0, 0.0).astype(jnp.bfloat16)
        tails = tail_ref[...].reshape(peers * geo.tail, LANES)
        tails_ref[...] = dot(back, tails).astype(jnp.bfloat16)

    for part, out_ref in enumerate((keys_ref, values_ref)):
        out_ref[...] = jnp.zeros_like(out_ref)
        halves = [part * 2 + half for half in range(HD // LANES)]
        tails = jnp.concatenate(
            [tails_ref[pl.ds(pl.multiple_of((step * 4 + c) * peers, SUB), peers), :] for c in halves],
            axis=1,
        )
        for q in range(geo.joins):
            rows = jnp.concatenate(
                [
                    slab_ref[
                        q * geo.join : (q + 1) * geo.join, c * main : (c + 1) * main, :
                    ].reshape(width, LANES)
                    for c in halves
                ],
                axis=1,
            )
            placed = dot(pick_ref[q, :, 0:width], rows)
            placed = placed + dot(pick_ref[q, :, width : width + peers], tails)
            out_ref[pl.ds(lows[q], geo.window), :] += placed.astype(jnp.bfloat16)


def unpack(geo, slot, received):
    head_rows = 4 * geo.main
    tail_block = geo.chunks * geo.main // geo.tail
    out = jax.ShapeDtypeStruct((geo.slots, geo.features), jnp.bfloat16)
    return pl.pallas_call(
        functools.partial(unpack_kernel, geo),
        grid=(geo.heads,),
        in_specs=[
            pl.BlockSpec(memory_space=pltpu.SMEM),
            pl.BlockSpec((geo.peers, head_rows, LANES), lambda t: (0, t, 0)),
            pl.BlockSpec((geo.peers, geo.tail, LANES), lambda t: (0, tail_block, 0)),
        ],
        out_specs=[pl.BlockSpec((geo.slots, HD), lambda t: (0, t))] * 2,
        out_shape=[out, out],
        scratch_shapes=[
            pltpu.VMEM((geo.joins, geo.window, geo.join * geo.main + geo.peers), jnp.bfloat16),
            pltpu.VMEM((geo.chunks * geo.peers, LANES), jnp.bfloat16),
        ],
        compiler_params=pltpu.CompilerParams(vmem_limit_bytes=VMEM_LIMIT),
        cost_estimate=pl.CostEstimate(
            flops=4 * geo.joins * geo.window * 256 * geo.features,
            bytes_accessed=4 * received.size,
            transcendentals=0,
        ),
    )(slot, received, received)


def merge(one, two):
    half = HD + LANES // 2
    peak_one, peak_two = one[..., HD : HD + 1], two[..., HD : HD + 1]
    peak = jnp.maximum(peak_one, peak_two)
    rescale_one, rescale_two = jnp.exp(peak_one - peak), jnp.exp(peak_two - peak)
    mixed = one * rescale_one + two * rescale_two
    lane = lax.broadcasted_iota(jnp.int32, one.shape, len(one.shape) - 1)
    return jnp.where((lane >= HD) & (lane < half), peak, mixed)


def on_device(
    cache_keys, cache_values, keep_flags, drop_weight, req_blocks, queries, new_keys, new_values,
    out_weight,
):
    peers = lax.axis_size("seq")
    me = lax.axis_index("seq")
    row_count, features = cache_keys.shape
    block_count = row_count // BLOCK
    geo = Geometry(peers, block_count, features)
    req_count = queries.shape[0]
    keep = keep_flags.reshape(block_count, BLOCK)
    weight = drop_weight.reshape(block_count, BLOCK)

    kept_count = jnp.sum(keep, axis=1)
    kept_all = lax.all_to_all(
        jnp.broadcast_to(kept_count[None, :], (peers, block_count)),
        "seq", split_axis=0, concat_axis=0, tiled=True,
    )

    request_ends = jnp.cumsum(req_blocks)
    first = (request_ends - req_blocks - me * block_count)[:, None]
    last = (request_ends - me * block_count)[:, None]
    packed, part = pack(geo, keep, weight, first, last, queries, cache_keys, cache_values)

    counts = jnp.sum(kept_all, axis=1) + block_count
    starts = jnp.cumsum(counts) - counts
    my_start = lax.dynamic_slice(starts, (me,), (1,)) % peers
    sent = turn(geo, my_start, packed)
    received = lax.all_to_all(sent, "seq", split_axis=0, concat_axis=0, tiled=True)
    slot = (starts + (me - starts) % peers) // peers
    packed_keys, packed_values = unpack(geo, slot, received)

    sizes = kept_all.reshape(-1) + 1
    ends = jnp.cumsum(sizes)
    rank = jnp.arange(geo.slots, dtype=jnp.int32) * peers + me
    block = jnp.sum((rank[:, None] >= ends[None, :]).astype(jnp.int32), axis=1)
    folds = rank[:, None] == (ends - 1)[None, :]
    block_bias = jnp.log((BLOCK + 1 - sizes).astype(jnp.float32))
    packed_bias = jnp.sum(jnp.where(folds, block_bias[None, :], 0.0), axis=1).astype(jnp.bfloat16)
    owner = jnp.sum((block[:, None] >= request_ends[None, :]).astype(jnp.int32), axis=1)
    packed_request = jnp.where(rank < ends[-1], owner, -1)

    distance = 1
    while distance < peers:
        pairs = [(i, i ^ distance) for i in range(peers)]
        part = merge(part, lax.ppermute(part, "seq", pairs))
        distance *= 2
    heads = geo.heads
    peak_score, softmax_total = part[..., HD], part[..., HD + LANES // 2]
    weighted = part[..., :HD]
    score_scale = 1.0 / jnp.sqrt(jnp.float32(HD))
    query_heads = queries.reshape(req_count, heads, HD)
    own_score = (
        jnp.einsum(
            "rhd,rhd->hr",
            query_heads,
            new_keys.reshape(req_count, heads, HD),
            preferred_element_type=jnp.float32,
        )
        * score_scale
    )
    final_peak = jnp.maximum(peak_score, own_score)
    rescale_old = jnp.exp(peak_score - final_peak)
    own_prob = jnp.exp(own_score - final_peak)
    new_value_heads = jnp.transpose(new_values.reshape(req_count, heads, HD), (1, 0, 2)).astype(
        jnp.float32
    )
    softmax_total = softmax_total * rescale_old + own_prob
    weighted = weighted * rescale_old[:, :, None] + own_prob[:, :, None] * new_value_heads
    attention_heads = weighted / softmax_total[:, :, None]
    attention = (
        jnp.transpose(attention_heads, (1, 0, 2))
        .reshape(req_count, heads * HD)
        .astype(jnp.bfloat16)
    )
    partial_output = jnp.dot(attention, out_weight, preferred_element_type=jnp.float32)
    layer_output = lax.psum_scatter(partial_output, "tp", scatter_dimension=0, tiled=True).astype(
        jnp.bfloat16
    )
    return (packed_keys, packed_values, packed_bias, packed_request, layer_output)


def solution(mesh):
    in_specs = (
        P("seq", "tp"),
        P("seq", "tp"),
        P("seq"),
        P("seq"),
        P(),
        P(None, "tp"),
        P(None, "tp"),
        P(None, "tp"),
        P("tp", "seq"),
    )
    out_specs = (P("seq", "tp"), P("seq", "tp"), P("seq"), P("seq"), P("tp", "seq"))
    return jax.shard_map(
        on_device, mesh=mesh, in_specs=in_specs, out_specs=out_specs, check_vma=False
    )
```

profile of v0, /device:TPU:12, one launch (start us, length us, event | category | flops | bytes accessed | tf_op | source)
XLA Modules:
  0.0 275.4 jit_solution(764134655374641215)
XLA Ops:
  0.6 0.0 copy-start
  0.6 0.8 bitcast_reduce_fusion
  1.5 0.6 broadcast_in_dim.67
  2.1 7.2 %all-to-all-start = ((s32[16,1,16]{2,1,0:T(1,128)}), s32[16,1,16]{2,1,0:T(1,128)S(1)}, u32[]{:S(2)}, u32[]{:S(2)}) async-start(s32[16,1,16]{2,1,0:T(1,128)} %broadcast_in_dim.67), calls=%async_computation | async-start | bytes 16384 | tf_op jit(solution)/shard_map/all_to_all | solution.py:347
  9.3 0.7 copy.28
  10.1 0.7 broadcast_subtract_fusion
  10.8 0.7 subtract_bitcast_fusion
  11.4 0.7 copy.29.first_ref
  12.1 16.6 %shard_map.128 = (bf16[16,1040,128]{2,1,0:T(8,128)(2,1)}, f32[4,12,384]{2,1,0:T(8,128)}) custom-call(s32[16,128]{1,0:T(8,128)} %bitcast.34, s32[16,128]{1,0:T(8,128)} %bitcast.36, s32[12,1]{1,0:T(8,128)} %copy.29.first_ref, s32[12,1]{1,0:T(8,128)} %get-tuple-element.36.last_ref, bf16[12,1024]{1,0:T(8,128)(2,1)} %query_ref.1, bf16[2048,1024]{1,0:T(8,128)(2,1)} %key_ref.1, ...), custom_call_target="tpu_custom_call" | custom-call | flops 4831838208 | bytes 12582912 | tf_op jit(solution)/shard_map/pallas_call | solution.py:186
  28.7 0.0 all-to-all-done
  28.7 0.4 add_reduce_fusion
  29.1 0.1 copy.27
  29.2 0.1 reduce.2
  29.3 0.6 and_select_fusion
  30.0 0.6 dynamic_slice.3
  32.5 130.3 %shard_map.129 = bf16[16,1040,128]{2,1,0:T(8,128)(2,1)} custom-call(s32[1]{0:T(128)S(6)} %select_n.45.start_ref, bf16[16,1040,128]{2,1,0:T(8,128)(2,1)} %get-tuple-element.9.packed_ref), custom_call_target="tpu_custom_call" | custom-call | bytes 8519680 | tf_op jit(solution)/shard_map/pallas_call | solution.py:234
  162.8 0.0 copy-start.1
  162.8 0.0 copy-start.2
  162.8 0.0 copy-start.3
  162.8 0.0 copy-start.4
  162.8 0.0 copy-start.5
  162.9 7.1 %all-to-all-start.1 = ((bf16[16,1040,128]{2,1,0:T(8,128)(2,1)}), bf16[16,1040,128]{2,1,0:T(8,128)(2,1)}, u32[]{:S(2)}, u32[]{:S(2)}) async-start(bf16[16,1040,128]{2,1,0:T(8,128)(2,1)} %shard_map.129), calls=%async_computation.1 | async-start | bytes 8519680 | tf_op jit(solution)/shard_map/all_to_all | solution.py:361
  169.9 0.0 copy-done.1
  169.9 1.5 collective-permute-start
  171.4 0.0 copy-done.2
  171.5 0.0 copy-done.3
  171.5 0.1 fusion.3
  171.6 0.1 copy.38
  171.7 0.0 copy-done.5
  171.8 0.6 dynamic-slice
  173.0 0.1 add.88
  173.1 0.3 reduce-window.27
  173.4 0.1 slice.43
  173.5 0.1 slice_reduce_fusion.2
  173.6 0.1 broadcast_add_fusion
  173.7 0.6 slice.45
  174.3 0.4 convert_reduce_fusion
  174.7 0.1 convert_reduce_fusion.1
  174.8 9.9 %collective-permute-done = f32[4,12,384]{2,1,0:T(8,128)S(1)} collective-permute-done((f32[4,12,384]{2,1,0:T(8,128)S(1)}, f32[4,12,384]{2,1,0:T(8,128)S(1)}, u32[]{:S(2)}, u32[]{:S(2)}) %collective-permute-start) | collective-permute-done | bytes 73760 | tf_op jit(solution)/shard_map/ppermute | solution.py:378
  184.7 0.1 fusion.10
  184.8 0.1 add_select_fusion.3
  184.9 0.6 collective-permute-start.1
  185.6 1.2 compare_select_fusion
  186.8 6.6 %collective-permute-done.1 = f32[4,12,384]{2,1,0:T(8,128)S(1)} collective-permute-done((f32[4,12,384]{2,1,0:T(8,128)S(1)}, f32[4,12,384]{2,1,0:T(8,128)S(1)}, u32[]{:S(2)}, u32[]{:S(2)}) %collective-permute-start.1) | collective-permute-done | bytes 73760 | tf_op jit(solution)/shard_map/ppermute | solution.py:378
  193.4 0.1 fusion.11
  193.6 0.1 add_select_fusion.2
  193.7 2.6 collective-permute-start.2
  196.3 0.1 log.11
  196.3 45.6 %collective-permute-done.2 = f32[4,12,384]{2,1,0:T(8,128)S(1)} collective-permute-done((f32[4,12,384]{2,1,0:T(8,128)S(1)}, f32[4,12,384]{2,1,0:T(8,128)S(1)}, u32[]{:S(2)}, u32[]{:S(2)}) %collective-permute-start.2) | collective-permute-done | bytes 73760 | tf_op jit(solution)/shard_map/ppermute | solution.py:378
  241.9 0.1 fusion.12
  242.1 0.1 add_select_fusion.1
  242.2 1.6 collective-permute-start.3
  243.8 1.0 select_reduce_fusion
  244.8 20.4 %collective-permute-done.3 = f32[4,12,384]{2,1,0:T(8,128)S(1)} collective-permute-done((f32[4,12,384]{2,1,0:T(8,128)S(1)}, f32[4,12,384]{2,1,0:T(8,128)S(1)}, u32[]{:S(2)}, u32[]{:S(2)}) %collective-permute-start.3) | collective-permute-done | bytes 73760 | tf_op jit(solution)/shard_map/ppermute | solution.py:378
  265.2 0.1 fusion.13
  265.3 0.1 add_select_fusion
  265.4 0.2 slice_reduce_fusion
  265.6 0.1 fusion.4
  265.7 0.0 copy-done
  265.7 0.2 fusion.16
  265.9 2.5 all-reduce
  268.4 0.6 dynamic-slice_convert_fusion
  269.0 0.0 all-to-all-done.1.slab_ref.tail_ref
  269.0 6.4 %shard_map.130 = (bf16[1040,1024]{1,0:T(8,128)(2,1)}, bf16[1040,1024]{1,0:T(8,128)(2,1)}) custom-call(s32[16]{0:T(128)} %get-tuple-element.34.slot_ref, bf16[16,1040,128]{2,1,0:T(8,128)(2,1)} %all-to-all-done.1.slab_ref.tail_ref, bf16[16,1040,128]{2,1,0:T(8,128)(2,1)} %all-to-all-done.1.slab_ref.tail_ref), custom_call_target="tpu_custom_call" | custom-call | flops 1207959552 | bytes 8519680 | tf_op jit(solution)/shard_map/pallas_call | solution.py:300
  (15 shorter events, 0.3 us)
Async XLA Ops:
  0.6 265.1 %copy-start = (bf16[1024,128]{1,0:T(8,128)(2,1)S(1)}, bf16[1024,128]{1,0:T(8,128)(2,1)}, u32[]{:S(2)}) copy-start(bf16[1024,128]{1,0:T(8,128)(2,1)} %param.17) | copy-start | bytes 786436
  2.1 26.6 %all-to-all-start = ((s32[16,1,16]{2,1,0:T(1,128)}), s32[16,1,16]{2,1,0:T(1,128)S(1)}, u32[]{:S(2)}, u32[]{:S(2)}) async-start(s32[16,1,16]{2,1,0:T(1,128)} %broadcast_in_dim.67), calls=%async_computation | async-start | bytes 16384 | tf_op jit(solution)/shard_map/all_to_all | solution.py:347
  162.8 7.1 %copy-start.1 = (f32[4,12,384]{2,1,0:T(8,128)S(1)}, f32[4,12,384]{2,1,0:T(8,128)}, u32[]{:S(2)}) copy-start(f32[4,12,384]{2,1,0:T(8,128)} %get-tuple-element.12) | copy-start | bytes 221188
  162.8 8.6 %copy-start.2 = (bf16[12,1024]{1,0:T(8,128)(2,1)S(1)}, bf16[12,1024]{1,0:T(8,128)(2,1)}, u32[]{:S(2)}) copy-start(bf16[12,1024]{1,0:T(8,128)(2,1)} %query_ref.1) | copy-start | bytes 73732
  162.8 8.7 %copy-start.3 = (bf16[12,1024]{1,0:T(8,128)(2,1)S(1)}, bf16[12,1024]{1,0:T(8,128)(2,1)}, u32[]{:S(2)}) copy-start(bf16[12,1024]{1,0:T(8,128)(2,1)} %param.15) | copy-start | bytes 73732
  162.8 8.9 %copy-start.4 = (bf16[12,1024]{1,0:T(8,128)(2,1)S(1)}, bf16[12,1024]{1,0:T(8,128)(2,1)}, u32[]{:S(2)}) copy-start(bf16[12,1024]{1,0:T(8,128)(2,1)} %param.16) | copy-start | bytes 73732
  162.8 8.9 %copy-start.5 = (u32[32]{0:T(128)S(1)}, u32[32]{0:T(128)}, u32[]{:S(2)}) copy-start(u32[32]{0:T(128)} %constant.77) | copy-start | bytes 388
  162.9 106.1 %all-to-all-start.1 = ((bf16[16,1040,128]{2,1,0:T(8,128)(2,1)}), bf16[16,1040,128]{2,1,0:T(8,128)(2,1)}, u32[]{:S(2)}, u32[]{:S(2)}) async-start(bf16[16,1040,128]{2,1,0:T(8,128)(2,1)} %shard_map.129), calls=%async_computation.1 | async-start | bytes 8519680 | tf_op jit(solution)/shard_map/all_to_all | solution.py:361
  169.9 14.8 %collective-permute-start = (f32[4,12,384]{2,1,0:T(8,128)S(1)}, f32[4,12,384]{2,1,0:T(8,128)S(1)}, u32[]{:S(2)}, u32[]{:S(2)}) collective-permute-start(f32[4,12,384]{2,1,0:T(8,128)S(1)} %copy-done.1), channel_id=1, source_target_pairs={{0,2},{2,0},{4,6},{6,4},{8,10},{10,8},{12,14},{14,12},{16,18},{18,... | collective-permute-start | bytes 221192 | tf_op jit(solution)/shard_map/ppermute | solution.py:378
  184.9 8.5 %collective-permute-start.1 = (f32[4,12,384]{2,1,0:T(8,128)S(1)}, f32[4,12,384]{2,1,0:T(8,128)S(1)}, u32[]{:S(2)}, u32[]{:S(2)}) collective-permute-start(f32[4,12,384]{2,1,0:T(8,128)S(1)} %add_select_fusion.3), channel_id=1, source_target_pairs={{0,4},{2,6},{4,0},{6,2},{8,12},{10,14},{12,8},{14,10},{16,20},{18,... | collective-permute-start | bytes 221192 | tf_op jit(solution)/shard_map/ppermute | solution.py:378
  193.7 48.3 %collective-permute-start.2 = (f32[4,12,384]{2,1,0:T(8,128)S(1)}, f32[4,12,384]{2,1,0:T(8,128)S(1)}, u32[]{:S(2)}, u32[]{:S(2)}) collective-permute-start(f32[4,12,384]{2,1,0:T(8,128)S(1)} %add_select_fusion.2), channel_id=1, source_target_pairs={{0,8},{2,10},{4,12},{6,14},{8,0},{10,2},{12,4},{14,6},{16,24},{18,... | collective-permute-start | bytes 221192 | tf_op jit(solution)/shard_map/ppermute | solution.py:378
  242.2 23.0 %collective-permute-start.3 = (f32[4,12,384]{2,1,0:T(8,128)S(1)}, f32[4,12,384]{2,1,0:T(8,128)S(1)}, u32[]{:S(2)}, u32[]{:S(2)}) collective-permute-start(f32[4,12,384]{2,1,0:T(8,128)S(1)} %add_select_fusion.1), channel_id=1, source_target_pairs={{0,16},{2,18},{4,20},{6,22},{8,24},{10,26},{12,28},{14,30},{16,0},... | collective-permute-start | bytes 221192 | tf_op jit(solution)/shard_map/ppermute | solution.py:378
where the time goes:
time: 280 us; the launch traced here: 275 us
  Pallas kernels  153 us (55%)
  waiting for transfers between devices  82.6 us (30%)
  starting transfers between devices  20.6 us (7%)
  other arithmetic  7.63 us (3%)
  local copies, waits for them, and re-layouts  5.2 us (2%)
  between operations  3.48 us (1%)
    pallas_call x1, Pallas kernels, turn(): pl.pallas_call(functools.partial(turn_kernel, geo), in_specs=[pl.BlockSpe...  130 us
    ppermute x4, waiting for transfers between devices, on_device(): part = merge(part, lax.ppermute(part, 'seq', pairs))  82.6 us
    pallas_call x1, Pallas kernels, pack(): pl.pallas_call(functools.partial(pack_kernel, geo), grid=(geo.heads,), in...  16.6 us
    all_to_all x1, starting transfers between devices, on_device(): lax.all_to_all(jnp.broadcast_to(kept_count[None, :], (peers, block_count)...  7.17 us
    all_to_all x1, starting transfers between devices, on_device(): lax.all_to_all(sent, 'seq', split_axis=0, concat_axis=0, tiled=True)  7.06 us
    pallas_call x1, Pallas kernels, unpack(): pl.pallas_call(functools.partial(unpack_kernel, geo), grid=(geo.heads,),...  6.4 us
    ppermute x4, starting transfers between devices, on_device(): part = merge(part, lax.ppermute(part, 'seq', pairs))  6.34 us
  transfers between devices with their start and end apart: 6, of which 4 were waited for; matrix products, arithmetic and copies ran while one was open for 4% of the time, Pallas kernels for 6%

commit v1 on v0

--- a/solution.py
+++ b/solution.py
@@ -233,10 +233,11 @@
 def turn(geo, start, packed):
     return pl.pallas_call(
         functools.partial(turn_kernel, geo),
-        in_specs=[pl.BlockSpec(memory_space=pltpu.SMEM), pl.BlockSpec(memory_space=pl.ANY)],
+        in_specs=[pl.BlockSpec(memory_space=pltpu.SMEM), pl.BlockSpec(memory_space=pltpu.VMEM)],
         out_specs=pl.BlockSpec(memory_space=pl.ANY),
         out_shape=jax.ShapeDtypeStruct(packed.shape, packed.dtype),
         scratch_shapes=[pltpu.SemaphoreType.DMA((geo.peers,))],
+        compiler_params=pltpu.CompilerParams(vmem_limit_bytes=VMEM_LIMIT),
         cost_estimate=pl.CostEstimate(flops=0, bytes_accessed=2 * packed.size * 2, transcendentals=0),
     )(start, packed)
 

time: 280 us -> 155 us (0.55)
  the two profiles are of different devices: /device:TPU:12 before, /device:TPU:5 now
where the time goes in v1:
time: 155 us; the launch traced here: 154 us
  waiting for transfers between devices  86.5 us (56%)
  Pallas kernels  27.4 us (18%)
  starting transfers between devices  19.9 us (13%)
  other arithmetic  7.63 us (5%)
  local copies, waits for them, and re-layouts  5.2 us (3%)
  blocking collectives  3.9 us (3%)
  between operations  3.48 us (2%)
    ppermute x4, waiting for transfers between devices, on_device(): part = merge(part, lax.ppermute(part, 'seq', pairs))  86.5 us
    pallas_call x1, Pallas kernels, pack(): pl.pallas_call(functools.partial(pack_kernel, geo), grid=(geo.heads,), in...  16.6 us
    all_to_all x1, starting transfers between devices, on_device(): lax.all_to_all(jnp.broadcast_to(kept_count[None, :], (peers, block_count)...  6.72 us
    ppermute x4, starting transfers between devices, on_device(): part = merge(part, lax.ppermute(part, 'seq', pairs))  6.64 us
    all_to_all x1, starting transfers between devices, on_device(): lax.all_to_all(sent, 'seq', split_axis=0, concat_axis=0, tiled=True)  6.5 us
    pallas_call x1, Pallas kernels, unpack(): pl.pallas_call(functools.partial(unpack_kernel, geo), grid=(geo.heads,),...  6.4 us
    pallas_call x1, Pallas kernels, turn(): pl.pallas_call(functools.partial(turn_kernel, geo), in_specs=[pl.BlockSpe...  4.35 us
    unnamed x1, blocking collectives  3.9 us
  transfers between devices with their start and end apart: 6, of which 4 were waited for; matrix products, arithmetic and copies ran while one was open for 6% of the time, Pallas kernels for 11%

profile of v1, /device:TPU:5, one launch (start us, length us, event | category | flops | bytes accessed | tf_op | source)
XLA Modules:
  0.0 154.1 jit_solution(17113925408471393733)
XLA Ops:
  0.6 0.0 copy-start
  0.6 0.8 bitcast_reduce_fusion
  1.5 0.6 broadcast_in_dim.67
  2.1 6.7 %all-to-all-start = ((s32[16,1,16]{2,1,0:T(1,128)}), s32[16,1,16]{2,1,0:T(1,128)S(1)}, u32[]{:S(2)}, u32[]{:S(2)}) async-start(s32[16,1,16]{2,1,0:T(1,128)} %broadcast_in_dim.67), calls=%async_computation | async-start | bytes 16384 | tf_op jit(solution)/shard_map/all_to_all | solution.py:348
  8.8 0.7 copy.28
  9.6 0.7 broadcast_subtract_fusion
  10.3 0.7 subtract_bitcast_fusion
  11.0 0.7 copy.29.first_ref
  11.7 16.6 %shard_map.128 = (bf16[16,1040,128]{2,1,0:T(8,128)(2,1)}, f32[4,12,384]{2,1,0:T(8,128)}) custom-call(s32[16,128]{1,0:T(8,128)} %bitcast.34, s32[16,128]{1,0:T(8,128)} %bitcast.36, s32[12,1]{1,0:T(8,128)} %copy.29.first_ref, s32[12,1]{1,0:T(8,128)} %get-tuple-element.36.last_ref, bf16[12,1024]{1,0:T(8,128)(2,1)} %query_ref.1, bf16[2048,1024]{1,0:T(8,128)(2,1)} %key_ref.1, ...), custom_call_target="tpu_custom_call" | custom-call | flops 4831838208 | bytes 12582912 | tf_op jit(solution)/shard_map/pallas_call | solution.py:186
  28.3 0.0 all-to-all-done
  28.3 0.4 add_reduce_fusion
  28.7 0.1 copy.27
  28.8 0.1 reduce.2
  28.9 0.6 and_select_fusion
  29.5 0.6 dynamic_slice.3
  32.0 4.4 %shard_map.129 = bf16[16,1040,128]{2,1,0:T(8,128)(2,1)} custom-call(s32[1]{0:T(128)S(6)} %select_n.45.start_ref, bf16[16,1040,128]{2,1,0:T(8,128)(2,1)} %get-tuple-element.9.packed_ref), custom_call_target="tpu_custom_call" | custom-call | bytes 8519680 | tf_op jit(solution)/shard_map/pallas_call | solution.py:234
  36.4 0.0 copy-start.1
  36.4 0.0 copy-start.2
  36.4 0.0 copy-start.3
  36.4 0.0 copy-start.4
  36.5 0.0 copy-start.5
  36.5 6.5 %all-to-all-start.1 = ((bf16[16,1040,128]{2,1,0:T(8,128)(2,1)}), bf16[16,1040,128]{2,1,0:T(8,128)(2,1)}, u32[]{:S(2)}, u32[]{:S(2)}) async-start(bf16[16,1040,128]{2,1,0:T(8,128)(2,1)} %shard_map.129), calls=%async_computation.1 | async-start | bytes 8519680 | tf_op jit(solution)/shard_map/all_to_all | solution.py:362
  43.0 0.0 copy-done.1
  43.0 1.2 collective-permute-start
  44.2 0.0 copy-done.2
  44.2 0.0 copy-done.3
  44.3 0.1 fusion.3
  44.4 0.1 copy.38
  44.5 0.0 copy-done.4
  44.5 0.0 copy-done.5
  44.5 0.6 dynamic-slice
  45.8 0.1 add.88
  45.9 0.3 reduce-window.27
  46.2 0.1 slice.43
  46.3 0.1 slice_reduce_fusion.2
  46.4 0.1 broadcast_add_fusion
  46.5 0.6 slice.45
  47.1 0.4 convert_reduce_fusion
  47.5 0.1 convert_reduce_fusion.1
  47.6 12.2 %collective-permute-done = f32[4,12,384]{2,1,0:T(8,128)S(1)} collective-permute-done((f32[4,12,384]{2,1,0:T(8,128)S(1)}, f32[4,12,384]{2,1,0:T(8,128)S(1)}, u32[]{:S(2)}, u32[]{:S(2)}) %collective-permute-start) | collective-permute-done | bytes 73760 | tf_op jit(solution)/shard_map/ppermute | solution.py:379
  59.8 0.1 fusion.10
  59.9 0.1 add_select_fusion.3
  60.0 0.1 collective-permute-start.1
  60.1 1.3 compare_select_fusion
  61.3 3.6 %collective-permute-done.1 = f32[4,12,384]{2,1,0:T(8,128)S(1)} collective-permute-done((f32[4,12,384]{2,1,0:T(8,128)S(1)}, f32[4,12,384]{2,1,0:T(8,128)S(1)}, u32[]{:S(2)}, u32[]{:S(2)}) %collective-permute-start.1) | collective-permute-done | bytes 73760 | tf_op jit(solution)/shard_map/ppermute | solution.py:379
  64.9 0.1 fusion.11
  65.0 0.1 add_select_fusion.2
  65.2 0.3 collective-permute-start.2
  65.5 0.1 log.11
  65.6 47.7 %collective-permute-done.2 = f32[4,12,384]{2,1,0:T(8,128)S(1)} collective-permute-done((f32[4,12,384]{2,1,0:T(8,128)S(1)}, f32[4,12,384]{2,1,0:T(8,128)S(1)}, u32[]{:S(2)}, u32[]{:S(2)}) %collective-permute-start.2) | collective-permute-done | bytes 73760 | tf_op jit(solution)/shard_map/ppermute | solution.py:379
  113.3 0.1 fusion.12
  113.4 0.1 add_select_fusion.1
  113.5 5.0 %collective-permute-start.3 = (f32[4,12,384]{2,1,0:T(8,128)S(1)}, f32[4,12,384]{2,1,0:T(8,128)S(1)}, u32[]{:S(2)}, u32[]{:S(2)}) collective-permute-start(f32[4,12,384]{2,1,0:T(8,128)S(1)} %add_select_fusion.1), channel_id=1, source_target_pairs={{0,16},{2,18},{4,20},{6,22},{8,24},{10,26},{12,28},{14,30},{16,0},... | collective-permute-start | bytes 221192 | tf_op jit(solution)/shard_map/ppermute | solution.py:379
  118.6 1.0 select_reduce_fusion
  119.5 22.9 %collective-permute-done.3 = f32[4,12,384]{2,1,0:T(8,128)S(1)} collective-permute-done((f32[4,12,384]{2,1,0:T(8,128)S(1)}, f32[4,12,384]{2,1,0:T(8,128)S(1)}, u32[]{:S(2)}, u32[]{:S(2)}) %collective-permute-start.3) | collective-permute-done | bytes 73760 | tf_op jit(solution)/shard_map/ppermute | solution.py:379
  142.5 0.1 fusion.13
  142.6 0.1 add_select_fusion
  142.7 0.2 slice_reduce_fusion
  142.9 0.1 fusion.4
  143.1 0.2 fusion.16
  143.2 3.9 %all-reduce = bf16[12,128]{1,0:T(8,128)(2,1)S(1)} all-reduce(f32[12,128]{1,0:T(8,128)S(1)} %fusion.16), channel_id=2, replica_groups=mesh['seq'=16,'tp'=2] {'tp'}, use_global_device_ids=true, to_apply=%region_9.10.clone | all-reduce | flops 1536 | bytes 9216
  147.1 0.6 dynamic-slice_convert_fusion
  147.7 0.0 all-to-all-done.1.slab_ref.tail_ref
  147.7 6.4 %shard_map.130 = (bf16[1040,1024]{1,0:T(8,128)(2,1)}, bf16[1040,1024]{1,0:T(8,128)(2,1)}) custom-call(s32[16]{0:T(128)} %get-tuple-element.34.slot_ref, bf16[16,1040,128]{2,1,0:T(8,128)(2,1)} %all-to-all-done.1.slab_ref.tail_ref, bf16[16,1040,128]{2,1,0:T(8,128)(2,1)} %all-to-all-done.1.slab_ref.tail_ref), custom_call_target="tpu_custom_call" | custom-call | flops 1207959552 | bytes 8519680 | tf_op jit(solution)/shard_map/pallas_call | solution.py:301
  (15 shorter events, 0.3 us)
Async XLA Ops:
  0.6 142.4 %copy-start = (bf16[1024,128]{1,0:T(8,128)(2,1)S(1)}, bf16[1024,128]{1,0:T(8,128)(2,1)}, u32[]{:S(2)}) copy-start(bf16[1024,128]{1,0:T(8,128)(2,1)} %param.17) | copy-start | bytes 786436
  2.1 26.2 %all-to-all-start = ((s32[16,1,16]{2,1,0:T(1,128)}), s32[16,1,16]{2,1,0:T(1,128)S(1)}, u32[]{:S(2)}, u32[]{:S(2)}) async-start(s32[16,1,16]{2,1,0:T(1,128)} %broadcast_in_dim.67), calls=%async_computation | async-start | bytes 16384 | tf_op jit(solution)/shard_map/all_to_all | solution.py:348
  36.4 6.6 %copy-start.1 = (f32[4,12,384]{2,1,0:T(8,128)S(1)}, f32[4,12,384]{2,1,0:T(8,128)}, u32[]{:S(2)}) copy-start(f32[4,12,384]{2,1,0:T(8,128)} %get-tuple-element.12) | copy-start | bytes 221188
  36.4 7.8 %copy-start.2 = (bf16[12,1024]{1,0:T(8,128)(2,1)S(1)}, bf16[12,1024]{1,0:T(8,128)(2,1)}, u32[]{:S(2)}) copy-start(bf16[12,1024]{1,0:T(8,128)(2,1)} %query_ref.1) | copy-start | bytes 73732
  36.4 7.8 %copy-start.3 = (bf16[12,1024]{1,0:T(8,128)(2,1)S(1)}, bf16[12,1024]{1,0:T(8,128)(2,1)}, u32[]{:S(2)}) copy-start(bf16[12,1024]{1,0:T(8,128)(2,1)} %param.15) | copy-start | bytes 73732
  36.4 8.0 %copy-start.4 = (bf16[12,1024]{1,0:T(8,128)(2,1)S(1)}, bf16[12,1024]{1,0:T(8,128)(2,1)}, u32[]{:S(2)}) copy-start(bf16[12,1024]{1,0:T(8,128)(2,1)} %param.16) | copy-start | bytes 73732
  36.5 8.1 %copy-start.5 = (u32[32]{0:T(128)S(1)}, u32[32]{0:T(128)}, u32[]{:S(2)}) copy-start(u32[32]{0:T(128)} %constant.77) | copy-start | bytes 388
  36.5 111.2 %all-to-all-start.1 = ((bf16[16,1040,128]{2,1,0:T(8,128)(2,1)}), bf16[16,1040,128]{2,1,0:T(8,128)(2,1)}, u32[]{:S(2)}, u32[]{:S(2)}) async-start(bf16[16,1040,128]{2,1,0:T(8,128)(2,1)} %shard_map.129), calls=%async_computation.1 | async-start | bytes 8519680 | tf_op jit(solution)/shard_map/all_to_all | solution.py:362
  43.0 16.8 %collective-permute-start = (f32[4,12,384]{2,1,0:T(8,128)S(1)}, f32[4,12,384]{2,1,0:T(8,128)S(1)}, u32[]{:S(2)}, u32[]{:S(2)}) collective-permute-start(f32[4,12,384]{2,1,0:T(8,128)S(1)} %copy-done.1), channel_id=1, source_target_pairs={{0,2},{2,0},{4,6},{6,4},{8,10},{10,8},{12,14},{14,12},{16,18},{18,... | collective-permute-start | bytes 221192 | tf_op jit(solution)/shard_map/ppermute | solution.py:379
  60.0 5.0 %collective-permute-start.1 = (f32[4,12,384]{2,1,0:T(8,128)S(1)}, f32[4,12,384]{2,1,0:T(8,128)S(1)}, u32[]{:S(2)}, u32[]{:S(2)}) collective-permute-start(f32[4,12,384]{2,1,0:T(8,128)S(1)} %add_select_fusion.3), channel_id=1, source_target_pairs={{0,4},{2,6},{4,0},{6,2},{8,12},{10,14},{12,8},{14,10},{16,20},{18,... | collective-permute-start | bytes 221192 | tf_op jit(solution)/shard_map/ppermute | solution.py:379
  65.2 48.2 %collective-permute-start.2 = (f32[4,12,384]{2,1,0:T(8,128)S(1)}, f32[4,12,384]{2,1,0:T(8,128)S(1)}, u32[]{:S(2)}, u32[]{:S(2)}) collective-permute-start(f32[4,12,384]{2,1,0:T(8,128)S(1)} %add_select_fusion.2), channel_id=1, source_target_pairs={{0,8},{2,10},{4,12},{6,14},{8,0},{10,2},{12,4},{14,6},{16,24},{18,... | collective-permute-start | bytes 221192 | tf_op jit(solution)/shard_map/ppermute | solution.py:379
  113.5 28.9 %collective-permute-start.3 = (f32[4,12,384]{2,1,0:T(8,128)S(1)}, f32[4,12,384]{2,1,0:T(8,128)S(1)}, u32[]{:S(2)}, u32[]{:S(2)}) collective-permute-start(f32[4,12,384]{2,1,0:T(8,128)S(1)} %add_select_fusion.1), channel_id=1, source_target_pairs={{0,16},{2,18},{4,20},{6,22},{8,24},{10,26},{12,28},{14,30},{16,0},... | collective-permute-start | bytes 221192 | tf_op jit(solution)/shard_map/ppermute | solution.py:379

commit v2 on v1

v2 whole, which is shorter than its diff:
```python
import functools

import jax
import jax.numpy as jnp
from jax import lax
from jax.experimental import pallas as pl
from jax.experimental.pallas import tpu as pltpu
from jax.sharding import PartitionSpec as P

HD = 256
BLOCK = 128
LANES = 128
SUB = 16
LEAST_KEPT = BLOCK // 4
MOST_KEPT = BLOCK // 2
LOW = -1e30
VMEM_LIMIT = 56 * 1024 * 1024


class Geometry:
    def __init__(self, peers, blocks, features):
        self.peers = peers
        self.blocks = blocks
        self.features = features
        self.heads = features // HD
        self.slots = blocks * (MOST_KEPT + 1)
        self.peer_rows = -(-self.slots // peers)
        self.groups = self.peer_rows // SUB
        self.main = self.groups * SUB
        self.chunks = 2 * features // LANES
        self.tail = -(-self.chunks // SUB) * SUB
        self.share = self.chunks // 2 * self.main
        self.group_rows = SUB * peers
        assert self.peer_rows == self.main + 1
        assert self.block_range(self.main * peers, self.slots - 1) == (blocks - 1, blocks)
        self.join = min(peers, max(1, 256 // self.main))
        self.joins = peers // self.join
        window = self.join * self.peer_rows + SUB - 1
        self.window = min(-(-window // SUB) * SUB, self.slots)
        assert self.slots % SUB == 0 and peers % self.join == 0

    def block_range(self, first, last):
        low = max(0, -(-(first - MOST_KEPT) // (MOST_KEPT + 1)))
        high = min(self.blocks - 1, last // (LEAST_KEPT + 1))
        return low, high + 1

    def ranges(self):
        rows = self.group_rows
        return [self.block_range(g * rows, (g + 1) * rows - 1) for g in range(self.groups)]

    def places(self):
        places = [0]
        for low, high in self.ranges():
            places.append(places[-1] + (high - low) * BLOCK)
        return places


def iota(shape, axis):
    return lax.broadcasted_iota(jnp.int32, shape, axis)


def dot(a, b, contract=((1,), (0,))):
    return lax.dot_general(a, b, (contract, ((), ())), preferred_element_type=jnp.float32)


def pack_kernel(geo, tails, keep_ref, weight_ref, cache_ref, *refs):
    step = pl.program_id(0)
    blocks, peers = geo.blocks, geo.peers
    if tails:
        end_refs, (main_ref, tail_ref, pick_ref, scale_ref) = refs[:2], refs[2:]
    else:
        main_ref, pick_ref, scale_ref = refs
    ranges = geo.ranges()
    places = geo.places()

    def flags():
        keep = keep_ref[...].reshape(blocks, BLOCK).astype(jnp.float32)
        weight = weight_ref[...].reshape(blocks, BLOCK).astype(jnp.float32)
        return keep, weight * (1.0 - keep)

    @pl.when(step == 0)
    def _():
        keep, dropped = flags()
        kept = jnp.sum(keep, axis=1, keepdims=True)
        inverse = 1.0 / jnp.sum(dropped, axis=1, keepdims=True)
        earlier = (iota((BLOCK, BLOCK), 0) < iota((BLOCK, BLOCK), 1)).astype(jnp.bfloat16)
        within = dot(keep.astype(jnp.bfloat16), earlier)
        before = (iota((blocks, blocks), 1) < iota((blocks, blocks), 0)).astype(jnp.bfloat16)
        sizes = jnp.broadcast_to(kept + 1.0, (blocks, BLOCK)).astype(jnp.bfloat16)
        base = dot(before, sizes)
        entry = jnp.where(keep > 0.0, base + within, -1.0).astype(jnp.int32)
        fold_entry = (base + kept).astype(jnp.int32)

        def select(index, low, high):
            scale = jnp.ones(index.shape, jnp.float32)
            picks = []
            for b in range(low, high):
                folds = index == fold_entry[b : b + 1, :]
                one = jnp.where(index == entry[b : b + 1, :], 1.0, 0.0)
                picked = jnp.where(folds, dropped[b : b + 1, :], one)
                picks.append(picked.astype(jnp.bfloat16))
                scale = jnp.where(folds, inverse[b : b + 1, :], scale)
            return picks, scale

        row = iota((geo.group_rows, BLOCK), 0)
        for g in range(geo.groups):
            index = (g * SUB + row % SUB) * peers + row // SUB
            picks, scale_ref[g, :, :] = select(index, *ranges[g])
            for i, picked in enumerate(picks):
                at = places[g] + i * BLOCK
                pick_ref[:, at : at + BLOCK] = picked
        if tails:
            index = geo.main * peers + iota((peers, BLOCK), 0)
            (picked,), scale = select(index, blocks - 1, blocks)
            left = []
            for end_ref in end_refs:
                rows = dot(picked, end_ref[...])
                for c in range(geo.chunks // 2):
                    left.append((rows[:, c * LANES : (c + 1) * LANES] * scale).astype(jnp.bfloat16))
            shape = (peers * geo.tail, geo.chunks * peers)
            row, col = iota(shape, 0), iota(shape, 1)
            wanted = row % geo.tail * peers + row // geo.tail
            turn = jnp.where(wanted == col, 1.0, 0.0).astype(jnp.bfloat16)
            rows = dot(turn, jnp.concatenate(left, axis=0)).astype(jnp.bfloat16)
            tail_ref[...] = rows.reshape(peers, geo.tail, LANES)

    for g in range(geo.groups):
        low, high = ranges[g]
        rows = dot(
            pick_ref[:, places[g] : places[g] + (high - low) * BLOCK],
            cache_ref[low * BLOCK : high * BLOCK, :],
        )
        for half in range(HD // LANES):
            chunk = rows[:, half * LANES : (half + 1) * LANES] * scale_ref[g]
            chunk = chunk.astype(jnp.bfloat16).reshape(peers, SUB, LANES)
            at = half * geo.main + g * SUB
            main_ref[:, at : at + SUB, :] = chunk


def attend_kernel(
    geo, keep_ref, weight_ref, first_ref, last_ref, query_ref, key_ref, value_ref,
    part_ref, fold_ref,
):
    step = pl.program_id(0)
    blocks = geo.blocks
    keep = keep_ref[...].reshape(blocks, BLOCK).astype(jnp.float32)
    weight = weight_ref[...].reshape(blocks, BLOCK).astype(jnp.float32)
    dropped = weight * (1.0 - keep)
    inverse = 1.0 / jnp.sum(dropped, axis=1, keepdims=True)

    @pl.when(step == 0)
    def _():
        for b in range(blocks):
            mine = iota((blocks, BLOCK), 0) == b
            fold_ref[:, b * BLOCK : (b + 1) * BLOCK] = jnp.where(
                mine, dropped[b : b + 1, :], 0.0
            ).astype(jnp.bfloat16)

    query = query_ref[...]
    first, last = first_ref[...], last_ref[...]
    requests = query.shape[0]
    score_scale = HD**-0.5
    folded_keys = (dot(fold_ref[...], key_ref[...]) * inverse).astype(jnp.bfloat16)
    folded_values = (dot(fold_ref[...], value_ref[...]) * inverse).astype(jnp.bfloat16)
    ones = jnp.ones((8, BLOCK), jnp.bfloat16)
    kept_lanes = dot(ones, keep.astype(jnp.bfloat16), ((1,), (1,)))[0:1, :]
    bias = jnp.log(BLOCK - kept_lanes).astype(jnp.bfloat16).astype(jnp.float32)
    fold_scores = dot(query, folded_keys, ((1,), (1,))) * score_scale + bias
    block = iota((requests, blocks), 1)
    fold_member = (block >= first) & (block < last)
    fold_scores = jnp.where(fold_member, fold_scores, LOW)
    scores = dot(query, key_ref[...], ((1,), (1,))) * score_scale
    lane_block = iota((requests, blocks * BLOCK), 1) // BLOCK
    kept_rows = jnp.concatenate(
        [jnp.broadcast_to(keep[b : b + 1, :], (requests, BLOCK)) for b in range(blocks)], axis=1
    )
    member = (lane_block >= first) & (lane_block < last) & (kept_rows > 0.0)
    scores = jnp.where(member, scores, LOW)
    peak = jnp.maximum(
        jnp.max(scores, axis=1, keepdims=True), jnp.max(fold_scores, axis=1, keepdims=True)
    )
    probs = jnp.where(member, jnp.exp(scores - peak), 0.0)
    fold_probs = jnp.where(fold_member, jnp.exp(fold_scores - peak), 0.0)
    total = jnp.sum(probs, axis=1, keepdims=True) + jnp.sum(fold_probs, axis=1, keepdims=True)
    mixed = dot(probs.astype(jnp.bfloat16), value_ref[...]) + dot(
        fold_probs.astype(jnp.bfloat16), folded_values
    )
    part_ref[0, :, 0:HD] = mixed
    part_ref[0, :, HD:] = jnp.where(iota((requests, LANES), 1) < LANES // 2, peak, total)


def whole(*shape):
    return pl.BlockSpec(shape, lambda t: (0,) * len(shape))


def pack(geo, keep, weight, cache, ends=()):
    rows = cache.shape[0]
    width = geo.places()[-1]
    end_block = geo.blocks - 1
    out_specs = [pl.BlockSpec((geo.peers, 2 * geo.main, LANES), lambda t: (0, t, 0))]
    out_shape = [jax.ShapeDtypeStruct((geo.peers, geo.share, LANES), jnp.bfloat16)]
    if ends:
        out_specs.append(whole(geo.peers, geo.tail, LANES))
        out_shape.append(jax.ShapeDtypeStruct((geo.peers, geo.tail, LANES), jnp.bfloat16))
    return pl.pallas_call(
        functools.partial(pack_kernel, geo, bool(ends)),
        grid=(geo.heads,),
        in_specs=[whole(rows), whole(rows), pl.BlockSpec((rows, HD), lambda t: (0, t))]
        + [pl.BlockSpec((BLOCK, geo.features), lambda t: (end_block, 0))] * len(ends),
        out_specs=out_specs,
        out_shape=out_shape,
        scratch_shapes=[
            pltpu.VMEM((geo.group_rows, width), jnp.bfloat16),
            pltpu.VMEM((geo.groups, geo.group_rows, BLOCK), jnp.float32),
        ],
        compiler_params=pltpu.CompilerParams(vmem_limit_bytes=VMEM_LIMIT),
        cost_estimate=pl.CostEstimate(
            flops=2 * geo.group_rows * width * geo.features,
            bytes_accessed=3 * rows * geo.features,
            transcendentals=0,
        ),
    )(keep, weight, cache, *ends)


def attend(geo, keep, weight, first, last, queries, cache_keys, cache_values):
    rows = cache_keys.shape[0]
    requests = queries.shape[0]
    return pl.pallas_call(
        functools.partial(attend_kernel, geo),
        grid=(geo.heads,),
        in_specs=[
            whole(rows),
            whole(rows),
            whole(requests, 1),
            whole(requests, 1),
            pl.BlockSpec((requests, HD), lambda t: (0, t)),
            pl.BlockSpec((rows, HD), lambda t: (0, t)),
            pl.BlockSpec((rows, HD), lambda t: (0, t)),
        ],
        out_specs=pl.BlockSpec((1, requests, HD + LANES), lambda t: (t, 0, 0)),
        out_shape=jax.ShapeDtypeStruct((geo.heads, requests, HD + LANES), jnp.float32),
        scratch_shapes=[pltpu.VMEM((geo.blocks, rows), jnp.bfloat16)],
        compiler_params=pltpu.CompilerParams(vmem_limit_bytes=VMEM_LIMIT),
        cost_estimate=pl.CostEstimate(
            flops=8 * rows * requests * geo.features,
            bytes_accessed=2 * rows * geo.features * 2,
            transcendentals=rows * requests * geo.heads,
        ),
    )(keep, weight, first, last, queries, cache_keys, cache_values)


def my_start(kept, me):
    return jnp.sum(jnp.where(iota(kept.shape, 0) < me, kept + 1, 0))


def turn_kernel(geo, kept_ref, *refs):
    main_ref, tail_refs = refs[0], refs[1:-4]
    sent_ref, held_ref, in_sems, out_sems = refs[-4:]
    me = lax.axis_index("seq")
    peers, share = geo.peers, geo.share
    arrivals = []
    for p in range(peers):
        held = held_ref.at[p]
        copies = [pltpu.make_async_copy(main_ref.at[p], held.at[0:share], in_sems.at[0, p])]
        for tail_ref in tail_refs:
            tail = held.at[share : share + geo.tail]
            copies.append(pltpu.make_async_copy(tail_ref.at[p], tail, in_sems.at[1, p]))
        for copy in copies:
            copy.start()
        arrivals.append(copies)
    start = my_start(kept_ref[...], me)
    departures = []
    for p in range(peers):
        device = lax.rem(start + p, peers)
        for copy in arrivals[p]:
            copy.wait()
        departures.append(
            pltpu.make_async_copy(held_ref.at[p], sent_ref.at[device], out_sems.at[p])
        )
        departures[p].start()
    for copy in departures:
        copy.wait()


def turn(geo, kept, main, tail=None):
    tails = [] if tail is None else [tail]
    shape = (geo.peers, geo.share + len(tails) * geo.tail, LANES)
    size = geo.peers * geo.share * LANES
    return pl.pallas_call(
        functools.partial(turn_kernel, geo),
        in_specs=[pl.BlockSpec(memory_space=pltpu.VMEM)]
        + [pl.BlockSpec(memory_space=pl.ANY)] * (1 + len(tails)),
        out_specs=pl.BlockSpec(memory_space=pl.ANY),
        out_shape=jax.ShapeDtypeStruct(shape, jnp.bfloat16),
        scratch_shapes=[
            pltpu.VMEM(shape, jnp.bfloat16),
            pltpu.SemaphoreType.DMA((2, geo.peers)),
            pltpu.SemaphoreType.DMA((geo.peers,)),
        ],
        compiler_params=pltpu.CompilerParams(vmem_limit_bytes=VMEM_LIMIT),
        cost_estimate=pl.CostEstimate(flops=0, bytes_accessed=4 * size, transcendentals=0),
    )(kept, main, *tails)


def unpack_kernel(geo, part, slot_ref, slab_ref, tail_ref, out_ref, pick_ref, tails_ref):
    peers, main = geo.peers, geo.main
    step = pl.program_id(0)
    width = geo.join * main
    halves = HD // LANES
    lows = []
    for q in range(geo.joins):
        low = jnp.minimum(slot_ref[q * geo.join] // SUB * SUB, geo.slots - geo.window)
        lows.append(pl.multiple_of(low, SUB))

    @pl.when(step == 0)
    def _():
        for q in range(geo.joins):
            lane = iota((1, width), 1)
            target = lane % main
            last = jnp.full((1, peers), -1, jnp.int32)
            for j in range(geo.join):
                at = slot_ref[q * geo.join + j] - lows[q]
                target = target + jnp.where(lane // main == j, at, 0)
                last = jnp.where(iota((1, peers), 1) == q * geo.join + j, at + main, last)
            picked = jnp.where(iota((geo.window, width), 0) == target, 1.0, 0.0)
            pick_ref[q, :, 0:width] = picked.astype(jnp.bfloat16)
            picked = jnp.where(iota((geo.window, peers), 0) == last, 1.0, 0.0)
            pick_ref[q, :, width : width + peers] = picked.astype(jnp.bfloat16)
        share = geo.chunks // 2
        shape = (share * peers, peers * geo.tail)
        row, col = iota(shape, 0), iota(shape, 1)
        wanted = row % peers * geo.tail + row // peers + part * share
        back = jnp.where(wanted == col, 1.0, 0.0).astype(jnp.bfloat16)
        tails = tail_ref[...].reshape(peers * geo.tail, LANES)
        tails_ref[...] = dot(back, tails).astype(jnp.bfloat16)

    out_ref[...] = jnp.zeros_like(out_ref)
    tails = jnp.concatenate(
        [
            tails_ref[pl.ds(pl.multiple_of((step * halves + c) * peers, SUB), peers), :]
            for c in range(halves)
        ],
        axis=1,
    )
    for q in range(geo.joins):
        sources = slice(q * geo.join, (q + 1) * geo.join)
        rows = [
            slab_ref[sources, c * main : (c + 1) * main, :].reshape(width, LANES)
            for c in range(halves)
        ]
        placed = dot(pick_ref[q, :, 0:width], jnp.concatenate(rows, axis=1))
        placed = placed + dot(pick_ref[q, :, width : width + peers], tails)
        out_ref[pl.ds(lows[q], geo.window), :] += placed.astype(jnp.bfloat16)


def unpack(geo, part, slot, slabs, tail):
    head_rows = HD // LANES * geo.main
    tail_block = geo.share // geo.tail
    return pl.pallas_call(
        functools.partial(unpack_kernel, geo, part),
        grid=(geo.heads,),
        in_specs=[
            pl.BlockSpec(memory_space=pltpu.SMEM),
            pl.BlockSpec((geo.peers, head_rows, LANES), lambda t: (0, t, 0)),
            pl.BlockSpec((geo.peers, geo.tail, LANES), lambda t: (0, tail_block, 0)),
        ],
        out_specs=pl.BlockSpec((geo.slots, HD), lambda t: (0, t)),
        out_shape=jax.ShapeDtypeStruct((geo.slots, geo.features), jnp.bfloat16),
        scratch_shapes=[
            pltpu.VMEM((geo.joins, geo.window, geo.join * geo.main + geo.peers), jnp.bfloat16),
            pltpu.VMEM((geo.chunks // 2 * geo.peers, LANES), jnp.bfloat16),
        ],
        compiler_params=pltpu.CompilerParams(vmem_limit_bytes=VMEM_LIMIT),
        cost_estimate=pl.CostEstimate(
            flops=2 * geo.joins * geo.window * 256 * geo.features,
            bytes_accessed=4 * geo.peers * geo.share * LANES,
            transcendentals=0,
        ),
    )(slot, slabs, tail)


def merge(one, two):
    half = HD + LANES // 2
    peak_one, peak_two = one[..., HD : HD + 1], two[..., HD : HD + 1]
    peak = jnp.maximum(peak_one, peak_two)
    rescale_one, rescale_two = jnp.exp(peak_one - peak), jnp.exp(peak_two - peak)
    mixed = one * rescale_one + two * rescale_two
    lane = lax.broadcasted_iota(jnp.int32, one.shape, len(one.shape) - 1)
    return jnp.where((lane >= HD) & (lane < half), peak, mixed)


def on_device(
    cache_keys, cache_values, keep_flags, drop_weight, req_blocks, queries, new_keys, new_values,
    out_weight,
):
    peers = lax.axis_size("seq")
    me = lax.axis_index("seq")
    row_count, features = cache_keys.shape
    block_count = row_count // BLOCK
    geo = Geometry(peers, block_count, features)
    req_count = queries.shape[0]
    kept_count = jnp.sum(keep_flags.reshape(block_count, BLOCK), axis=1)
    kept_all = lax.all_to_all(
        jnp.broadcast_to(kept_count[None, :], (peers, block_count)),
        "seq", split_axis=0, concat_axis=0, tiled=True,
    )

    main, tail = pack(geo, keep_flags, drop_weight, cache_keys, (cache_keys, cache_values))
    sent = turn(geo, kept_all, main, tail)
    tied = (sent, keep_flags, drop_weight, kept_all, req_blocks)
    sent, keep_flags, drop_weight, kept_all, req_blocks = lax.optimization_barrier(tied)
    keys = lax.all_to_all(sent, "seq", split_axis=0, concat_axis=0, tiled=True)

    request_ends = jnp.cumsum(req_blocks)
    first = (request_ends - req_blocks - me * block_count)[:, None]
    last = (request_ends - me * block_count)[:, None]
    part = attend(geo, keep_flags, drop_weight, first, last, queries, cache_keys, cache_values)
    (main,) = pack(geo, keep_flags, drop_weight, cache_values)
    sent = turn(geo, kept_all, main)
    distance = 1
    while distance < peers:
        if distance == peers // 2:
            part, sent = lax.optimization_barrier((part, sent))
        pairs = [(i, i ^ distance) for i in range(peers)]
        part = merge(part, lax.ppermute(part, "seq", pairs))
        distance *= 2
    part, sent = lax.optimization_barrier((part, sent))
    values = lax.all_to_all(sent, "seq", split_axis=0, concat_axis=0, tiled=True)

    counts = jnp.sum(kept_all, axis=1) + block_count
    starts = jnp.cumsum(counts) - counts
    slot = (starts + (me - starts) % peers) // peers
    packed_keys = unpack(geo, 0, slot, keys, keys)
    packed_values = unpack(geo, 1, slot, values, keys)

    sizes = kept_all.reshape(-1) + 1
    ends = jnp.cumsum(sizes)
    rank = jnp.arange(geo.slots, dtype=jnp.int32) * peers + me
    block = jnp.sum((rank[:, None] >= ends[None, :]).astype(jnp.int32), axis=1)
    folds = rank[:, None] == (ends - 1)[None, :]
    block_bias = jnp.log((BLOCK + 1 - sizes).astype(jnp.float32))
    packed_bias = jnp.sum(jnp.where(folds, block_bias[None, :], 0.0), axis=1).astype(jnp.bfloat16)
    owner = jnp.sum((block[:, None] >= request_ends[None, :]).astype(jnp.int32), axis=1)
    packed_request = jnp.where(rank < ends[-1], owner, -1)

    heads = geo.heads
    peak_score, softmax_total = part[..., HD], part[..., HD + LANES // 2]
    weighted = part[..., :HD]
    score_scale = 1.0 / jnp.sqrt(jnp.float32(HD))
    query_heads = queries.reshape(req_count, heads, HD)
    own_score = (
        jnp.einsum(
            "rhd,rhd->hr",
            query_heads,
            new_keys.reshape(req_count, heads, HD),
            preferred_element_type=jnp.float32,
        )
        * score_scale
    )
    final_peak = jnp.maximum(peak_score, own_score)
    rescale_old = jnp.exp(peak_score - final_peak)
    own_prob = jnp.exp(own_score - final_peak)
    new_value_heads = jnp.transpose(new_values.reshape(req_count, heads, HD), (1, 0, 2)).astype(
        jnp.float32
    )
    softmax_total = softmax_total * rescale_old + own_prob
    weighted = weighted * rescale_old[:, :, None] + own_prob[:, :, None] * new_value_heads
    attention_heads = weighted / softmax_total[:, :, None]
    attention = (
        jnp.transpose(attention_heads, (1, 0, 2))
        .reshape(req_count, heads * HD)
        .astype(jnp.bfloat16)
    )
    partial_output = jnp.dot(attention, out_weight, preferred_element_type=jnp.float32)
    layer_output = lax.psum_scatter(partial_output, "tp", scatter_dimension=0, tiled=True).astype(
        jnp.bfloat16
    )
    return (packed_keys, packed_values, packed_bias, packed_request, layer_output)


def solution(mesh):
    in_specs = (
        P("seq", "tp"),
        P("seq", "tp"),
        P("seq"),
        P("seq"),
        P(),
        P(None, "tp"),
        P(None, "tp"),
        P(None, "tp"),
        P("tp", "seq"),
    )
    out_specs = (P("seq", "tp"), P("seq", "tp"), P("seq"), P("seq"), P("tp", "seq"))
    return jax.shard_map(
        on_device, mesh=mesh, in_specs=in_specs, out_specs=out_specs, check_vma=False
    )
```

time: 155 us -> 141 us (0.910)
  the two profiles are of different devices: /device:TPU:5 before, /device:TPU:12 now
where the time goes in v2:
time: 141 us; the launch traced here: 140 us
  waiting for transfers between devices  55 us (39%)
  Pallas kernels  40.9 us (29%)
  starting transfers between devices  25.6 us (18%)
  other arithmetic  8.25 us (6%)
  local copies, waits for them, and re-layouts  5.94 us (4%)
  blocking collectives  2.48 us (2%)
  between operations  1.57 us (1%)
    all_to_all x1, waiting for transfers between devices, on_device(): lax.all_to_all(sent, 'seq', split_axis=0, concat_axis=0, tiled=True)  31.4 us
    ppermute x4, waiting for transfers between devices, on_device(): part = merge(part, lax.ppermute(part, 'seq', pairs))  22.6 us
    pallas_call x2, Pallas kernels, pack(): pl.pallas_call(functools.partial(pack_kernel, geo, bool(ends)), grid=(geo...  15.2 us
    pallas_call x2, Pallas kernels, unpack(): pl.pallas_call(functools.partial(unpack_kernel, geo, part), grid=(geo.hea...  10.2 us
    pallas_call x1, Pallas kernels, attend(): pl.pallas_call(functools.partial(attend_kernel, geo), grid=(geo.heads,),...  8.47 us
    all_to_all x1, starting transfers between devices, on_device(): lax.all_to_all(jnp.broadcast_to(kept_count[None, :], (peers, block_count)...  7.17 us
    pallas_call x2, Pallas kernels, turn(): pl.pallas_call(functools.partial(turn_kernel, geo), in_specs=[pl.BlockSpe...  6.99 us
    all_to_all x1, starting transfers between devices, on_device(): keys = lax.all_to_all(sent, 'seq', split_axis=0, concat_axis=0, tiled=True)  6.89 us
  transfers between devices with their start and end apart: 7, of which 6 were waited for; matrix products, arithmetic and copies ran while one was open for 8% of the time, Pallas kernels for 23%

profile of v2, /device:TPU:12, one launch (start us, length us, event | category | flops | bytes accessed | tf_op | source)
XLA Modules:
  0.0 140.0 jit_solution(16189944145775032085)
XLA Ops:
  0.6 0.0 copy-start
  0.6 0.8 bitcast_reduce_fusion
  1.5 0.6 broadcast_in_dim.67
  2.1 7.2 %all-to-all-start = ((s32[16,1,16]{2,1,0:T(1,128)}), s32[16,1,16]{2,1,0:T(1,128)S(1)}, u32[]{:S(2)}, u32[]{:S(2)}) async-start(s32[16,1,16]{2,1,0:T(1,128)} %broadcast_in_dim.67), calls=%async_computation | async-start | bytes 16384 | tf_op jit(solution)/shard_map/all_to_all | solution.py:403
  9.3 7.7 %shard_map.128 = (bf16[16,512,128]{2,1,0:T(8,128)(2,1)}, bf16[16,16,128]{2,1,0:T(8,128)(2,1)}) custom-call(s32[2048]{0:T(1024)} %keep_ref.3, s32[2048]{0:T(1024)} %weight_ref.3, bf16[2048,1024]{1,0:T(8,128)(2,1)} %key_ref.1, bf16[2048,1024]{1,0:T(8,128)(2,1)} %key_ref.1, bf16[2048,1024]{1,0:T(8,128)(2,1)} %cache_ref.3), custom_call_target="tpu_custom_call" | custom-call | flops 2348810240 | bytes 6291456 | tf_op jit(solution)/shard_map/pallas_call | solution.py:205
  17.0 0.0 copy-start.2
  17.0 0.6 copy-done.2
  17.6 3.5 %shard_map.129 = bf16[16,528,128]{2,1,0:T(8,128)(2,1)} custom-call(s32[16,16]{1,0:T(8,128)} %bitcast.34, bf16[16,512,128]{2,1,0:T(8,128)(2,1)} %get-tuple-element.16.refs_0_, bf16[16,16,128]{2,1,0:T(8,128)(2,1)} %get-tuple-element.17.refs_1_), custom_call_target="tpu_custom_call" | custom-call | bytes 4194304 | tf_op jit(solution)/shard_map/pallas_call | solution.py:289
  21.1 6.9 %all-to-all-start.1 = ((bf16[16,528,128]{2,1,0:T(8,128)(2,1)}), bf16[16,528,128]{2,1,0:T(8,128)(2,1)S(1)}, u32[]{:S(2)}, u32[]{:S(2)}) async-start(bf16[16,528,128]{2,1,0:T(8,128)(2,1)} %shard_map.129), calls=%async_computation.1 | async-start | bytes 4325376 | tf_op jit(solution)/shard_map/all_to_all | solution.py:412
  28.0 0.1 copy.28
  28.1 0.7 broadcast_subtract_fusion
  28.9 0.7 copy.29.first_ref
  29.6 8.5 %shard_map.131 = f32[4,12,384]{2,1,0:T(8,128)} custom-call(s32[2048]{0:T(1024)} %keep_ref.3, s32[2048]{0:T(1024)} %weight_ref.3, s32[12,1]{1,0:T(8,128)} %copy.29.first_ref, s32[12,1]{1,0:T(8,128)} %get-tuple-element.48.last_ref, bf16[12,1024]{1,0:T(8,128)(2,1)} %query_ref.1, bf16[2048,1024]{1,0:T(8,128)(2,1)} %key_ref.1, bf16[2048,1024]{1,0:T(8,128)(2,1)} %cache_ref.3), custom_call_target="tpu_custom_call" | custom-call | flops 201326592 | bytes 8388608 | tf_op jit(solution)/shard_map/pallas_call | solution.py:228
  38.0 1.5 %collective-permute-start = (f32[4,12,384]{2,1,0:T(8,128)}, f32[4,12,384]{2,1,0:T(8,128)S(1)}, u32[]{:S(2)}, u32[]{:S(2)}) collective-permute-start(f32[4,12,384]{2,1,0:T(8,128)} %shard_map.131), channel_id=1, source_target_pairs={{0,2},{2,0},{4,6},{6,4},{8,10},{10,8},{12,14},{14,12},{16,18},{18,... | collective-permute-start | bytes 221192 | tf_op jit(solution)/shard_map/ppermute | solution.py:425
  39.5 4.4 %collective-permute-done = f32[4,12,384]{2,1,0:T(8,128)S(1)} collective-permute-done((f32[4,12,384]{2,1,0:T(8,128)}, f32[4,12,384]{2,1,0:T(8,128)S(1)}, u32[]{:S(2)}, u32[]{:S(2)}) %collective-permute-start) | collective-permute-done | bytes 73760 | tf_op jit(solution)/shard_map/ppermute | solution.py:425
  43.9 0.9 fusion.10
  44.8 1.0 add_select_fusion.3
  45.8 0.1 collective-permute-start.1
  45.8 5.1 %collective-permute-done.1 = f32[4,12,384]{2,1,0:T(8,128)S(1)} collective-permute-done((f32[4,12,384]{2,1,0:T(8,128)S(1)}, f32[4,12,384]{2,1,0:T(8,128)S(1)}, u32[]{:S(2)}, u32[]{:S(2)}) %collective-permute-start.1) | collective-permute-done | bytes 73760 | tf_op jit(solution)/shard_map/ppermute | solution.py:425
  51.0 0.1 fusion.11
  51.1 0.1 add_select_fusion.2
  51.2 0.1 collective-permute-start.2
  51.3 7.6 %shard_map.132.refs_0_ = bf16[16,512,128]{2,1,0:T(8,128)(2,1)} custom-call(s32[2048]{0:T(1024)} %keep_ref.3, s32[2048]{0:T(1024)} %weight_ref.3, bf16[2048,1024]{1,0:T(8,128)(2,1)} %cache_ref.3), custom_call_target="tpu_custom_call" | custom-call | flops 2348810240 | bytes 6291456 | tf_op jit(solution)/shard_map/pallas_call | solution.py:205
  58.8 3.5 %shard_map.133 = bf16[16,512,128]{2,1,0:T(8,128)(2,1)} custom-call(s32[16,16]{1,0:T(8,128)} %bitcast.35, bf16[16,512,128]{2,1,0:T(8,128)(2,1)} %shard_map.132.refs_0_), custom_call_target="tpu_custom_call" | custom-call | bytes 4194304 | tf_op jit(solution)/shard_map/pallas_call | solution.py:289
  62.3 3.0 %collective-permute-done.2 = f32[4,12,384]{2,1,0:T(8,128)S(1)} collective-permute-done((f32[4,12,384]{2,1,0:T(8,128)S(1)}, f32[4,12,384]{2,1,0:T(8,128)S(1)}, u32[]{:S(2)}, u32[]{:S(2)}) %collective-permute-start.2) | collective-permute-done | bytes 73760 | tf_op jit(solution)/shard_map/ppermute | solution.py:425
  65.3 0.1 fusion.12
  65.4 0.1 add_select_fusion.1
  65.5 3.4 %collective-permute-start.3 = (f32[4,12,384]{2,1,0:T(8,128)S(1)}, f32[4,12,384]{2,1,0:T(8,128)S(1)}, u32[]{:S(2)}, u32[]{:S(2)}) collective-permute-start(f32[4,12,384]{2,1,0:T(8,128)S(1)} %add_select_fusion.1), channel_id=1, source_target_pairs={{0,16},{2,18},{4,20},{6,22},{8,24},{10,26},{12,28},{14,30},{16,0},... | collective-permute-start | bytes 221192 | tf_op jit(solution)/shard_map/ppermute | solution.py:425
  68.9 10.1 %collective-permute-done.3 = f32[4,12,384]{2,1,0:T(8,128)S(1)} collective-permute-done((f32[4,12,384]{2,1,0:T(8,128)S(1)}, f32[4,12,384]{2,1,0:T(8,128)S(1)}, u32[]{:S(2)}, u32[]{:S(2)}) %collective-permute-start.3) | collective-permute-done | bytes 73760 | tf_op jit(solution)/shard_map/ppermute | solution.py:425
  79.0 0.1 fusion.13
  79.1 0.1 add_select_fusion
  79.2 0.0 copy-start.5
  79.2 0.0 copy-start.6
  79.2 0.0 copy-start.8
  79.3 0.0 copy-start.3
  79.3 1.0 all-to-all-done.1.slab_ref.tail_ref
  80.3 1.3 copy-done.1
  81.6 6.5 %all-to-all-start.2 = ((bf16[16,512,128]{2,1,0:T(8,128)(2,1)}), bf16[16,512,128]{2,1,0:T(8,128)(2,1)}, u32[]{:S(2)}, u32[]{:S(2)}) async-start(bf16[16,512,128]{2,1,0:T(8,128)(2,1)} %shard_map.133), calls=%async_computation.2 | async-start | bytes 4194304 | tf_op jit(solution)/shard_map/all_to_all | solution.py:428
  88.2 0.1 fusion.3
  88.3 0.1 copy.38
  88.5 0.6 dynamic-slice
  89.7 0.1 broadcast_add_fusion
  89.8 0.1 copy.27
  90.0 0.1 reduce.1
  90.1 0.1 add.81
  90.2 0.3 reduce-window.27
  90.5 0.1 slice.51
  90.6 0.1 slice_reduce_fusion.2
  90.7 0.1 broadcast_add_fusion.1
  90.8 0.6 slice.53
  91.4 0.1 log.11
  91.5 0.4 convert_reduce_fusion
  91.9 0.1 convert_reduce_fusion.1
  92.0 1.0 select_reduce_fusion
  93.0 0.5 and_select_fusion.slot_ref
  93.5 1.2 compare_select_fusion
  94.7 0.2 slice_reduce_fusion
  94.9 0.1 fusion.4
  95.1 0.2 fusion.16
  95.2 2.5 %all-reduce = bf16[12,128]{1,0:T(8,128)(2,1)S(1)} all-reduce(f32[12,128]{1,0:T(8,128)S(1)} %fusion.16), channel_id=2, replica_groups=mesh['seq'=16,'tp'=2] {'tp'}, use_global_device_ids=true, to_apply=%region_9.10.clone | all-reduce | flops 1536 | bytes 9216
  97.7 0.6 dynamic-slice_convert_fusion
  98.3 5.1 %shard_map.130 = bf16[1040,1024]{1,0:T(8,128)(2,1)} custom-call(s32[16]{0:T(128)} %and_select_fusion.slot_ref, bf16[16,528,128]{2,1,0:T(8,128)(2,1)} %copy-done.1, bf16[16,528,128]{2,1,0:T(8,128)(2,1)} %copy-done.1), custom_call_target="tpu_custom_call" | custom-call | flops 603979776 | bytes 4194304 | tf_op jit(solution)/shard_map/pallas_call | solution.py:359
  103.4 31.4 %all-to-all-done.2.slab_ref = bf16[16,512,128]{2,1,0:T(8,128)(2,1)} async-done(((bf16[16,512,128]{2,1,0:T(8,128)(2,1)}), bf16[16,512,128]{2,1,0:T(8,128)(2,1)}, u32[]{:S(2)}, u32[]{:S(2)}) %all-to-all-start.2) | async-done | bytes 2097184 | tf_op jit(solution)/shard_map/all_to_all | solution.py:428
  134.9 5.1 %shard_map.134 = bf16[1040,1024]{1,0:T(8,128)(2,1)} custom-call(s32[16]{0:T(128)} %and_select_fusion.slot_ref, bf16[16,512,128]{2,1,0:T(8,128)(2,1)} %all-to-all-done.2.slab_ref, bf16[16,528,128]{2,1,0:T(8,128)(2,1)} %copy-done.1), custom_call_target="tpu_custom_call" | custom-call | flops 603979776 | bytes 4194304 | tf_op jit(solution)/shard_map/pallas_call | solution.py:359
  (26 shorter events, 0.3 us)
Async XLA Ops:
  0.6 94.4 %copy-start = (bf16[1024,128]{1,0:T(8,128)(2,1)S(1)}, bf16[1024,128]{1,0:T(8,128)(2,1)}, u32[]{:S(2)}) copy-start(bf16[1024,128]{1,0:T(8,128)(2,1)} %param.17) | copy-start | bytes 786436
  2.1 14.9 %all-to-all-start = ((s32[16,1,16]{2,1,0:T(1,128)}), s32[16,1,16]{2,1,0:T(1,128)S(1)}, u32[]{:S(2)}, u32[]{:S(2)}) async-start(s32[16,1,16]{2,1,0:T(1,128)} %broadcast_in_dim.67), calls=%async_computation | async-start | bytes 16384 | tf_op jit(solution)/shard_map/all_to_all | solution.py:403
  17.0 0.6 copy-start.2
  21.1 6.9 %copy-start.7 = (s32[12]{0:T(128)S(1)}, s32[12]{0:T(128)}, u32[]{:S(2)}) copy-start(s32[12]{0:T(128)} %param.13) | copy-start | bytes 148
  21.1 59.2 %all-to-all-start.1 = ((bf16[16,528,128]{2,1,0:T(8,128)(2,1)}), bf16[16,528,128]{2,1,0:T(8,128)(2,1)S(1)}, u32[]{:S(2)}, u32[]{:S(2)}) async-start(bf16[16,528,128]{2,1,0:T(8,128)(2,1)} %shard_map.129), calls=%async_computation.1 | async-start | bytes 4325376 | tf_op jit(solution)/shard_map/all_to_all | solution.py:412
  38.0 5.9 %collective-permute-start = (f32[4,12,384]{2,1,0:T(8,128)}, f32[4,12,384]{2,1,0:T(8,128)S(1)}, u32[]{:S(2)}, u32[]{:S(2)}) collective-permute-start(f32[4,12,384]{2,1,0:T(8,128)} %shard_map.131), channel_id=1, source_target_pairs={{0,2},{2,0},{4,6},{6,4},{8,10},{10,8},{12,14},{14,12},{16,18},{18,... | collective-permute-start | bytes 221192 | tf_op jit(solution)/shard_map/ppermute | solution.py:425
  45.8 5.2 %collective-permute-start.1 = (f32[4,12,384]{2,1,0:T(8,128)S(1)}, f32[4,12,384]{2,1,0:T(8,128)S(1)}, u32[]{:S(2)}, u32[]{:S(2)}) collective-permute-start(f32[4,12,384]{2,1,0:T(8,128)S(1)} %add_select_fusion.3), channel_id=1, source_target_pairs={{0,4},{2,6},{4,0},{6,2},{8,12},{10,14},{12,8},{14,10},{16,20},{18,... | collective-permute-start | bytes 221192 | tf_op jit(solution)/shard_map/ppermute | solution.py:425
  51.2 14.1 %collective-permute-start.2 = (f32[4,12,384]{2,1,0:T(8,128)S(1)}, f32[4,12,384]{2,1,0:T(8,128)S(1)}, u32[]{:S(2)}, u32[]{:S(2)}) collective-permute-start(f32[4,12,384]{2,1,0:T(8,128)S(1)} %add_select_fusion.2), channel_id=1, source_target_pairs={{0,8},{2,10},{4,12},{6,14},{8,0},{10,2},{12,4},{14,6},{16,24},{18,... | collective-permute-start | bytes 221192 | tf_op jit(solution)/shard_map/ppermute | solution.py:425
  65.5 13.5 %collective-permute-start.3 = (f32[4,12,384]{2,1,0:T(8,128)S(1)}, f32[4,12,384]{2,1,0:T(8,128)S(1)}, u32[]{:S(2)}, u32[]{:S(2)}) collective-permute-start(f32[4,12,384]{2,1,0:T(8,128)S(1)} %add_select_fusion.1), channel_id=1, source_target_pairs={{0,16},{2,18},{4,20},{6,22},{8,24},{10,26},{12,28},{14,30},{16,0},... | collective-permute-start | bytes 221192 | tf_op jit(solution)/shard_map/ppermute | solution.py:425
  79.2 8.9 %copy-start.4 = (bf16[12,1024]{1,0:T(8,128)(2,1)S(1)}, bf16[12,1024]{1,0:T(8,128)(2,1)}, u32[]{:S(2)}) copy-start(bf16[12,1024]{1,0:T(8,128)(2,1)} %query_ref.1) | copy-start | bytes 73732
  79.2 9.0 %copy-start.5 = (bf16[12,1024]{1,0:T(8,128)(2,1)S(1)}, bf16[12,1024]{1,0:T(8,128)(2,1)}, u32[]{:S(2)}) copy-start(bf16[12,1024]{1,0:T(8,128)(2,1)} %param.15) | copy-start | bytes 73732
  79.2 9.2 %copy-start.6 = (bf16[12,1024]{1,0:T(8,128)(2,1)S(1)}, bf16[12,1024]{1,0:T(8,128)(2,1)}, u32[]{:S(2)}) copy-start(bf16[12,1024]{1,0:T(8,128)(2,1)} %param.16) | copy-start | bytes 73732
  79.2 9.2 %copy-start.8 = (u32[32]{0:T(128)S(1)}, u32[32]{0:T(128)}, u32[]{:S(2)}) copy-start(u32[32]{0:T(128)} %constant.62) | copy-start | bytes 388
  79.3 10.5 %copy-start.3 = (s32[16,1,16]{2,1,0:T(1,128)S(1)}, s32[16,1,16]{2,1,0:T(1,128)}, u32[]{:S(2)}) copy-start(s32[16,1,16]{2,1,0:T(1,128)} %copy-done.2) | copy-start | bytes 3076
  80.3 1.4 copy-start.1
  81.6 53.2 %all-to-all-start.2 = ((bf16[16,512,128]{2,1,0:T(8,128)(2,1)}), bf16[16,512,128]{2,1,0:T(8,128)(2,1)}, u32[]{:S(2)}, u32[]{:S(2)}) async-start(bf16[16,512,128]{2,1,0:T(8,128)(2,1)} %shard_map.133), calls=%async_computation.2 | async-start | bytes 4194304 | tf_op jit(solution)/shard_map/all_to_all | solution.py:428

commit v3 on v2

--- a/solution.py
+++ b/solution.py
@@ -15,6 +15,7 @@
 MOST_KEPT = BLOCK // 2
 LOW = -1e30
 VMEM_LIMIT = 56 * 1024 * 1024
+VMEM_SMALL = 24 * 1024 * 1024
 
 
 class Geometry:
@@ -179,6 +180,7 @@
     peak = jnp.maximum(
         jnp.max(scores, axis=1, keepdims=True), jnp.max(fold_scores, axis=1, keepdims=True)
     )
+    peak = peak.astype(jnp.bfloat16).astype(jnp.float32)
     probs = jnp.where(member, jnp.exp(scores - peak), 0.0)
     fold_probs = jnp.where(fold_member, jnp.exp(fold_scores - peak), 0.0)
     total = jnp.sum(probs, axis=1, keepdims=True) + jnp.sum(fold_probs, axis=1, keepdims=True)
@@ -254,8 +256,10 @@
 
 
 def turn_kernel(geo, kept_ref, *refs):
-    main_ref, tail_refs = refs[0], refs[1:-4]
-    sent_ref, held_ref, in_sems, out_sems = refs[-4:]
+    main_ref, tail_refs = refs[0], refs[1:-6]
+    sent_ref, counts_ref, held_ref, counts_sem, in_sems, out_sems = refs[-6:]
+    counts = pltpu.make_async_copy(kept_ref, counts_ref, counts_sem)
+    counts.start()
     me = lax.axis_index("seq")
     peers, share = geo.peers, geo.share
     arrivals = []
@@ -268,7 +272,8 @@
         for copy in copies:
             copy.start()
         arrivals.append(copies)
-    start = my_start(kept_ref[...], me)
+    counts.wait()
+    start = my_start(counts_ref[...], me)
     departures = []
     for p in range(peers):
         device = lax.rem(start + p, peers)
@@ -288,12 +293,13 @@
     size = geo.peers * geo.share * LANES
     return pl.pallas_call(
         functools.partial(turn_kernel, geo),
-        in_specs=[pl.BlockSpec(memory_space=pltpu.VMEM)]
-        + [pl.BlockSpec(memory_space=pl.ANY)] * (1 + len(tails)),
+        in_specs=[pl.BlockSpec(memory_space=pl.ANY)] * (2 + len(tails)),
         out_specs=pl.BlockSpec(memory_space=pl.ANY),
         out_shape=jax.ShapeDtypeStruct(shape, jnp.bfloat16),
         scratch_shapes=[
+            pltpu.VMEM(kept.shape, jnp.int32),
             pltpu.VMEM(shape, jnp.bfloat16),
+            pltpu.SemaphoreType.DMA,
             pltpu.SemaphoreType.DMA((2, geo.peers)),
             pltpu.SemaphoreType.DMA((geo.peers,)),
         ],
@@ -302,81 +308,98 @@
     )(kept, main, *tails)
 
 
-def unpack_kernel(geo, part, slot_ref, slab_ref, tail_ref, out_ref, pick_ref, tails_ref):
-    peers, main = geo.peers, geo.main
-    step = pl.program_id(0)
-    width = geo.join * main
-    halves = HD // LANES
+def low_slots(geo, slot_ref):
     lows = []
     for q in range(geo.joins):
         low = jnp.minimum(slot_ref[q * geo.join] // SUB * SUB, geo.slots - geo.window)
         lows.append(pl.multiple_of(low, SUB))
-
-    @pl.when(step == 0)
-    def _():
-        for q in range(geo.joins):
-            lane = iota((1, width), 1)
-            target = lane % main
-            last = jnp.full((1, peers), -1, jnp.int32)
-            for j in range(geo.join):
-                at = slot_ref[q * geo.join + j] - lows[q]
-                target = target + jnp.where(lane // main == j, at, 0)
-                last = jnp.where(iota((1, peers), 1) == q * geo.join + j, at + main, last)
-            picked = jnp.where(iota((geo.window, width), 0) == target, 1.0, 0.0)
-            pick_ref[q, :, 0:width] = picked.astype(jnp.bfloat16)
-            picked = jnp.where(iota((geo.window, peers), 0) == last, 1.0, 0.0)
-            pick_ref[q, :, width : width + peers] = picked.astype(jnp.bfloat16)
-        share = geo.chunks // 2
+    return lows
+
+
+def plan_kernel(geo, slot_ref, tail_ref, pick_ref, last_ref, keys_ref, values_ref):
+    peers, main = geo.peers, geo.main
+    width = geo.join * main
+    lows = low_slots(geo, slot_ref)
+    for q in range(geo.joins):
+        lane = iota((1, width), 1)
+        target = lane % main
+        last = jnp.full((1, peers), -1, jnp.int32)
+        for j in range(geo.join):
+            at = slot_ref[q * geo.join + j] - lows[q]
+            target = target + jnp.where(lane // main == j, at, 0)
+            last = jnp.where(iota((1, peers), 1) == q * geo.join + j, at + main, last)
+        picked = jnp.where(iota((geo.window, width), 0) == target, 1.0, 0.0)
+        pick_ref[q, :, :] = picked.astype(jnp.bfloat16)
+        picked = jnp.where(iota((geo.window, peers), 0) == last, 1.0, 0.0)
+        last_ref[q, :, :] = picked.astype(jnp.bfloat16)
+    tails = tail_ref[...].reshape(peers * geo.tail, LANES)
+    share = geo.chunks // 2
+    for part, out_ref in enumerate((keys_ref, values_ref)):
         shape = (share * peers, peers * geo.tail)
         row, col = iota(shape, 0), iota(shape, 1)
         wanted = row % peers * geo.tail + row // peers + part * share
         back = jnp.where(wanted == col, 1.0, 0.0).astype(jnp.bfloat16)
-        tails = tail_ref[...].reshape(peers * geo.tail, LANES)
-        tails_ref[...] = dot(back, tails).astype(jnp.bfloat16)
-
+        rows = dot(back, tails).astype(jnp.bfloat16)
+        for c in range(share):
+            at = c * LANES
+            out_ref[:, at : at + LANES] = rows[c * peers : (c + 1) * peers, :]
+
+
+def plan(geo, slot, slabs):
+    tail_block = geo.share // geo.tail
+    picks = [(geo.joins, geo.window, n) for n in (geo.join * geo.main, geo.peers)]
+    shapes = picks + [(geo.peers, geo.features)] * 2
+    return pl.pallas_call(
+        functools.partial(plan_kernel, geo),
+        grid=(1,),
+        in_specs=[
+            pl.BlockSpec(memory_space=pltpu.SMEM),
+            pl.BlockSpec((geo.peers, geo.tail, LANES), lambda t: (0, tail_block, 0)),
+        ],
+        out_specs=[whole(*shape) for shape in shapes],
+        out_shape=[jax.ShapeDtypeStruct(shape, jnp.bfloat16) for shape in shapes],
+        compiler_params=pltpu.CompilerParams(vmem_limit_bytes=VMEM_SMALL),
+    )(slot, slabs)
+
+
+def unpack_kernel(geo, slot_ref, slab_ref, pick_ref, last_ref, tail_ref, out_ref):
+    main = geo.main
+    width = geo.join * main
+    lows = low_slots(geo, slot_ref)
     out_ref[...] = jnp.zeros_like(out_ref)
-    tails = jnp.concatenate(
-        [
-            tails_ref[pl.ds(pl.multiple_of((step * halves + c) * peers, SUB), peers), :]
-            for c in range(halves)
-        ],
-        axis=1,
-    )
     for q in range(geo.joins):
         sources = slice(q * geo.join, (q + 1) * geo.join)
         rows = [
             slab_ref[sources, c * main : (c + 1) * main, :].reshape(width, LANES)
-            for c in range(halves)
+            for c in range(out_ref.shape[1] // LANES)
         ]
-        placed = dot(pick_ref[q, :, 0:width], jnp.concatenate(rows, axis=1))
-        placed = placed + dot(pick_ref[q, :, width : width + peers], tails)
+        placed = dot(pick_ref[q], jnp.concatenate(rows, axis=1))
+        placed = placed + dot(last_ref[q], tail_ref[...])
         out_ref[pl.ds(lows[q], geo.window), :] += placed.astype(jnp.bfloat16)
 
 
-def unpack(geo, part, slot, slabs, tail):
-    head_rows = HD // LANES * geo.main
-    tail_block = geo.share // geo.tail
+def unpack(geo, slot, slabs, pick, last, tail):
+    tile = HD * (2 if geo.heads % 2 == 0 else 1)
+    tile_rows = tile // LANES * geo.main
     return pl.pallas_call(
-        functools.partial(unpack_kernel, geo, part),
-        grid=(geo.heads,),
+        functools.partial(unpack_kernel, geo),
+        grid=(geo.features // tile,),
         in_specs=[
             pl.BlockSpec(memory_space=pltpu.SMEM),
-            pl.BlockSpec((geo.peers, head_rows, LANES), lambda t: (0, t, 0)),
-            pl.BlockSpec((geo.peers, geo.tail, LANES), lambda t: (0, tail_block, 0)),
+            pl.BlockSpec((geo.peers, tile_rows, LANES), lambda t: (0, t, 0)),
+            whole(*pick.shape),
+            whole(*last.shape),
+            pl.BlockSpec((geo.peers, tile), lambda t: (0, t)),
         ],
-        out_specs=pl.BlockSpec((geo.slots, HD), lambda t: (0, t)),
+        out_specs=pl.BlockSpec((geo.slots, tile), lambda t: (0, t)),
         out_shape=jax.ShapeDtypeStruct((geo.slots, geo.features), jnp.bfloat16),
-        scratch_shapes=[
-            pltpu.VMEM((geo.joins, geo.window, geo.join * geo.main + geo.peers), jnp.bfloat16),
-            pltpu.VMEM((geo.chunks // 2 * geo.peers, LANES), jnp.bfloat16),
-        ],
-        compiler_params=pltpu.CompilerParams(vmem_limit_bytes=VMEM_LIMIT),
+        compiler_params=pltpu.CompilerParams(vmem_limit_bytes=VMEM_SMALL),
         cost_estimate=pl.CostEstimate(
             flops=2 * geo.joins * geo.window * 256 * geo.features,
             bytes_accessed=4 * geo.peers * geo.share * LANES,
             transcendentals=0,
         ),
-    )(slot, slabs, tail)
+    )(slot, slabs, pick, last, tail)
 
 
 def merge(one, two):
@@ -387,6 +410,21 @@
     mixed = one * rescale_one + two * rescale_two
     lane = lax.broadcasted_iota(jnp.int32, one.shape, len(one.shape) - 1)
     return jnp.where((lane >= HD) & (lane < half), peak, mixed)
+
+
+def narrow(part):
+    lane = lax.broadcasted_iota(jnp.int32, part.shape, len(part.shape) - 1)
+    high = part.astype(jnp.bfloat16)
+    low = (part - high.astype(jnp.float32)).astype(jnp.bfloat16)
+    return jnp.where(lane < HD + LANES * 3 // 4, high, low)
+
+
+def widen(part):
+    total = HD + LANES // 2
+    part = part.astype(jnp.float32)
+    lane = lax.broadcasted_iota(jnp.int32, part.shape, len(part.shape) - 1)
+    both = part[..., total : total + 1] + part[..., -1:]
+    return jnp.where(lane >= total, both, part)
 
 
 def on_device(
@@ -422,7 +460,10 @@
         if distance == peers // 2:
             part, sent = lax.optimization_barrier((part, sent))
         pairs = [(i, i ^ distance) for i in range(peers)]
-        part = merge(part, lax.ppermute(part, "seq", pairs))
+        if distance == peers // 2:
+            part = merge(part, widen(lax.ppermute(narrow(part), "seq", pairs)))
+        else:
+            part = merge(part, lax.ppermute(part, "seq", pairs))
         distance *= 2
     part, sent = lax.optimization_barrier((part, sent))
     values = lax.all_to_all(sent, "seq", split_axis=0, concat_axis=0, tiled=True)
@@ -430,8 +471,9 @@
     counts = jnp.sum(kept_all, axis=1) + block_count
     starts = jnp.cumsum(counts) - counts
     slot = (starts + (me - starts) % peers) // peers
-    packed_keys = unpack(geo, 0, slot, keys, keys)
-    packed_values = unpack(geo, 1, slot, values, keys)
+    pick, last, key_tails, value_tails = plan(geo, slot, keys)
+    packed_keys = unpack(geo, slot, keys, pick, last, key_tails)
+    packed_values = unpack(geo, slot, values, pick, last, value_tails)
 
     sizes = kept_all.reshape(-1) + 1
     ends = jnp.cumsum(sizes)

time: 141 us -> 136 us (0.965)
  Pallas kernels: 40.9 us -> 38.5 us
    ppermute x4 -> x3, waiting for transfers between devices: 22.6 us -> 12.7 us  [on_device(): part = merge(part, lax.ppermute(part, 'seq', pairs))]
    ppermute x0 -> x1, waiting for transfers between devices: none -> 7.97 us  [on_device(): part = merge(part, widen(lax.ppermute(narrow(part), 'seq', pairs)))]
    ppermute x4 -> x3, starting transfers between devices: 5.05 us -> 1.61 us  [on_device(): part = merge(part, lax.ppermute(part, 'seq', pairs))]
    ppermute x0 -> x1, starting transfers between devices: none -> 3.43 us  [on_device(): part = merge(part, widen(lax.ppermute(narrow(part), 'seq', pairs)))]
    pallas_call x2 -> x3, Pallas kernels: 10.2 us -> 8.09 us  [the longest x2 7.11 us: unpack(): pl.pallas_call(functools.partial(unpack_kernel, geo), grid=(geo.features...]
where the time goes in v3:
time: 136 us; the launch traced here: 135 us
  waiting for transfers between devices  54.6 us (40%)
  Pallas kernels  38.5 us (28%)
  starting transfers between devices  25.4 us (19%)
  other arithmetic  8.05 us (6%)
  local copies, waits for them, and re-layouts  4.59 us (3%)
  blocking collectives  2.48 us (2%)
  between operations  1.59 us (1%)
    all_to_all x1, waiting for transfers between devices, on_device(): lax.all_to_all(sent, 'seq', split_axis=0, concat_axis=0, tiled=True)  32.7 us
    pallas_call x2, Pallas kernels, pack(): pl.pallas_call(functools.partial(pack_kernel, geo, bool(ends)), grid=(geo...  15.2 us
    ppermute x3, waiting for transfers between devices, on_device(): part = merge(part, lax.ppermute(part, 'seq', pairs))  12.7 us
    pallas_call x1, Pallas kernels, attend(): pl.pallas_call(functools.partial(attend_kernel, geo), grid=(geo.heads,),...  8.48 us
    ppermute x1, waiting for transfers between devices, on_device(): part = merge(part, widen(lax.ppermute(narrow(part), 'seq', pairs)))  7.97 us
    all_to_all x1, starting transfers between devices, on_device(): lax.all_to_all(jnp.broadcast_to(kept_count[None, :], (peers, block_count)...  7.17 us
    pallas_call x2, Pallas kernels, unpack(): pl.pallas_call(functools.partial(unpack_kernel, geo), grid=(geo.features...  7.11 us
    all_to_all x1, starting transfers between devices, on_device(): keys = lax.all_to_all(sent, 'seq', split_axis=0, concat_axis=0, tiled=True)  6.92 us
  transfers between devices with their start and end apart: 7, of which 6 were waited for; matrix products, arithmetic and copies ran while one was open for 8% of the time, Pallas kernels for 23%

profile of v3, /device:TPU:12, one launch (start us, length us, event | category | flops | bytes accessed | tf_op | source)
XLA Modules:
  0.0 135.4 jit_solution(434746113834747932)
XLA Ops:
  0.6 0.0 copy-start
  0.6 0.8 bitcast_reduce_fusion
  1.5 0.6 broadcast_in_dim.74
  2.1 7.2 %all-to-all-start = ((s32[16,1,16]{2,1,0:T(1,128)}), s32[16,1,16]{2,1,0:T(1,128)S(1)}, u32[]{:S(2)}, u32[]{:S(2)}) async-start(s32[16,1,16]{2,1,0:T(1,128)} %broadcast_in_dim.74), calls=%async_computation | async-start | bytes 16384 | tf_op jit(solution)/shard_map/all_to_all | solution.py:441
  9.3 7.7 %shard_map.128 = (bf16[16,512,128]{2,1,0:T(8,128)(2,1)}, bf16[16,16,128]{2,1,0:T(8,128)(2,1)}) custom-call(s32[2048]{0:T(1024)} %keep_ref.3, s32[2048]{0:T(1024)} %weight_ref.3, bf16[2048,1024]{1,0:T(8,128)(2,1)} %key_ref.1, bf16[2048,1024]{1,0:T(8,128)(2,1)} %key_ref.1, bf16[2048,1024]{1,0:T(8,128)(2,1)} %cache_ref.3), custom_call_target="tpu_custom_call" | custom-call | flops 2348810240 | bytes 6291456 | tf_op jit(solution)/shard_map/pallas_call | solution.py:207
  17.0 0.0 copy-start.1
  17.0 0.6 copy-done.1
  17.6 3.5 %shard_map.129 = bf16[16,528,128]{2,1,0:T(8,128)(2,1)} custom-call(s32[16,16]{1,0:T(8,128)} %bitcast.34, bf16[16,512,128]{2,1,0:T(8,128)(2,1)} %get-tuple-element.20.refs_0_, bf16[16,16,128]{2,1,0:T(8,128)(2,1)} %get-tuple-element.21.refs_1_), custom_call_target="tpu_custom_call" | custom-call | bytes 4194304 | tf_op jit(solution)/shard_map/pallas_call | solution.py:294
  21.0 6.9 %all-to-all-start.1 = ((bf16[16,528,128]{2,1,0:T(8,128)(2,1)}), bf16[16,528,128]{2,1,0:T(8,128)(2,1)S(1)}, u32[]{:S(2)}, u32[]{:S(2)}) async-start(bf16[16,528,128]{2,1,0:T(8,128)(2,1)} %shard_map.129), calls=%async_computation.1 | async-start | bytes 4325376 | tf_op jit(solution)/shard_map/all_to_all | solution.py:450
  28.0 0.1 copy.28
  28.1 0.7 broadcast_subtract_fusion
  28.8 0.7 copy.29.first_ref
  29.5 8.5 %shard_map.132 = f32[4,12,384]{2,1,0:T(8,128)} custom-call(s32[2048]{0:T(1024)} %keep_ref.3, s32[2048]{0:T(1024)} %weight_ref.3, s32[12,1]{1,0:T(8,128)} %copy.29.first_ref, s32[12,1]{1,0:T(8,128)} %get-tuple-element.56.last_ref, bf16[12,1024]{1,0:T(8,128)(2,1)} %query_ref.1, bf16[2048,1024]{1,0:T(8,128)(2,1)} %key_ref.1, bf16[2048,1024]{1,0:T(8,128)(2,1)} %cache_ref.3), custom_call_target="tpu_custom_call" | custom-call | flops 201326592 | bytes 8388608 | tf_op jit(solution)/shard_map/pallas_call | solution.py:230
  38.0 1.5 %collective-permute-start = (f32[4,12,384]{2,1,0:T(8,128)}, f32[4,12,384]{2,1,0:T(8,128)S(1)}, u32[]{:S(2)}, u32[]{:S(2)}) collective-permute-start(f32[4,12,384]{2,1,0:T(8,128)} %shard_map.132), channel_id=1, source_target_pairs={{0,2},{2,0},{4,6},{6,4},{8,10},{10,8},{12,14},{14,12},{16,18},{18,... | collective-permute-start | bytes 221192 | tf_op jit(solution)/shard_map/ppermute | solution.py:466
  39.5 4.4 %collective-permute-done = f32[4,12,384]{2,1,0:T(8,128)S(1)} collective-permute-done((f32[4,12,384]{2,1,0:T(8,128)}, f32[4,12,384]{2,1,0:T(8,128)S(1)}, u32[]{:S(2)}, u32[]{:S(2)}) %collective-permute-start) | collective-permute-done | bytes 73760 | tf_op jit(solution)/shard_map/ppermute | solution.py:466
  43.9 0.9 fusion.12
  44.7 1.0 add_select_fusion.3
  45.7 0.1 collective-permute-start.1
  45.8 5.1 %collective-permute-done.1 = f32[4,12,384]{2,1,0:T(8,128)S(1)} collective-permute-done((f32[4,12,384]{2,1,0:T(8,128)S(1)}, f32[4,12,384]{2,1,0:T(8,128)S(1)}, u32[]{:S(2)}, u32[]{:S(2)}) %collective-permute-start.1) | collective-permute-done | bytes 73760 | tf_op jit(solution)/shard_map/ppermute | solution.py:466
  50.9 0.1 fusion.13
  51.0 0.1 add_select_fusion.2
  51.1 0.1 collective-permute-start.2
  51.2 7.6 %shard_map.133.refs_0_ = bf16[16,512,128]{2,1,0:T(8,128)(2,1)} custom-call(s32[2048]{0:T(1024)} %keep_ref.3, s32[2048]{0:T(1024)} %weight_ref.3, bf16[2048,1024]{1,0:T(8,128)(2,1)} %cache_ref.3), custom_call_target="tpu_custom_call" | custom-call | flops 2348810240 | bytes 6291456 | tf_op jit(solution)/shard_map/pallas_call | solution.py:207
  58.8 3.2 %shard_map.134 = bf16[16,512,128]{2,1,0:T(8,128)(2,1)} custom-call(s32[16,16]{1,0:T(8,128)} %bitcast.35, bf16[16,512,128]{2,1,0:T(8,128)(2,1)} %shard_map.133.refs_0_), custom_call_target="tpu_custom_call" | custom-call | bytes 4194304 | tf_op jit(solution)/shard_map/pallas_call | solution.py:294
  62.0 3.2 %collective-permute-done.2 = f32[4,12,384]{2,1,0:T(8,128)S(1)} collective-permute-done((f32[4,12,384]{2,1,0:T(8,128)S(1)}, f32[4,12,384]{2,1,0:T(8,128)S(1)}, u32[]{:S(2)}, u32[]{:S(2)}) %collective-permute-start.2) | collective-permute-done | bytes 73760 | tf_op jit(solution)/shard_map/ppermute | solution.py:466
  65.2 0.1 fusion.14
  65.3 0.1 add_select_fusion.1
  65.4 3.4 %collective-permute-start.3 = (bf16[4,12,384]{2,1,0:T(8,128)(2,1)S(1)}, bf16[4,12,384]{2,1,0:T(8,128)(2,1)S(1)}, u32[]{:S(2)}, u32[]{:S(2)}) collective-permute-start(bf16[4,12,384]{2,1,0:T(8,128)(2,1)S(1)} %fusion), channel_id=1, source_target_pairs={{0,16},{2,18},{4,20},{6,22},{8,24},{10,26},{12,28},{14,30},{16,0},... | collective-permute-start | bytes 110600 | tf_op jit(solution)/shard_map/ppermute | solution.py:464
  68.9 8.0 %collective-permute-done.3 = bf16[4,12,384]{2,1,0:T(8,128)(2,1)S(1)} collective-permute-done((bf16[4,12,384]{2,1,0:T(8,128)(2,1)S(1)}, bf16[4,12,384]{2,1,0:T(8,128)(2,1)S(1)}, u32[]{:S(2)}, u32[]{:S(2)}) %collective-permute-start.3) | collective-permute-done | bytes 36896 | tf_op jit(solution)/shard_map/ppermute | solution.py:464
  76.9 0.2 fusion.5
  77.0 0.1 broadcast_select_fusion
  77.1 0.1 fusion.15
  77.2 0.1 add_select_fusion
  77.3 0.0 copy-start.3
  77.4 0.0 copy-start.5
  77.4 0.0 copy-start.7
  77.4 1.3 all-to-all-done.1.tail_ref.slab_ref
  78.7 6.3 %all-to-all-start.2 = ((bf16[16,512,128]{2,1,0:T(8,128)(2,1)}), bf16[16,512,128]{2,1,0:T(8,128)(2,1)}, u32[]{:S(2)}, u32[]{:S(2)}) async-start(bf16[16,512,128]{2,1,0:T(8,128)(2,1)} %shard_map.134), calls=%async_computation.2 | async-start | bytes 4194304 | tf_op jit(solution)/shard_map/all_to_all | solution.py:469
  85.0 0.1 fusion.4
  85.1 0.1 copy.38
  85.2 0.6 dynamic-slice
  86.5 0.1 broadcast_add_fusion
  86.6 0.1 copy.27
  86.8 0.1 reduce.1
  86.9 0.1 add.85
  86.9 0.3 reduce-window.27
  87.3 0.1 slice.59
  87.4 0.1 slice_reduce_fusion.2
  87.5 0.1 broadcast_add_fusion.1
  87.6 0.6 slice.61
  88.2 0.1 log.11
  88.3 0.4 convert_reduce_fusion
  88.6 0.1 convert_reduce_fusion.1
  88.7 1.0 select_reduce_fusion
  89.8 1.2 compare_select_fusion
  91.0 0.2 slice_reduce_fusion
  91.2 0.1 fusion.6
  91.4 0.2 fusion.18
  91.5 2.5 %all-reduce = bf16[12,128]{1,0:T(8,128)(2,1)S(1)} all-reduce(f32[12,128]{1,0:T(8,128)S(1)} %fusion.18), channel_id=2, replica_groups=mesh['seq'=16,'tp'=2] {'tp'}, use_global_device_ids=true, to_apply=%region_9.10.clone | all-reduce | flops 1536 | bytes 9216
  94.0 0.6 dynamic-slice_convert_fusion
  94.6 1.0 shard_map.130
  95.6 3.3 %shard_map.131 = bf16[1040,1024]{1,0:T(8,128)(2,1)} custom-call(s32[16]{0:T(128)S(1)} %and_select_fusion.slot_ref, bf16[16,528,128]{2,1,0:T(8,128)(2,1)S(1)} %all-to-all-done.1.tail_ref.slab_ref, bf16[4,288,256]{2,1,0:T(8,128)(2,1)S(1)} %get-tuple-element.24.pick_ref, bf16[4,288,16]{2,1,0:T(8,128)(2,1)S(1)} %get-tuple-element.25.last_ref, ...), custom_call_target="tpu_custom_call" | custom-call | flops 603979776 | bytes 4194304 | tf_op jit(solution)/shard_map/pallas_call | solution.py:384
  98.9 32.7 %all-to-all-done.2.slab_ref = bf16[16,512,128]{2,1,0:T(8,128)(2,1)} async-done(((bf16[16,512,128]{2,1,0:T(8,128)(2,1)}), bf16[16,512,128]{2,1,0:T(8,128)(2,1)}, u32[]{:S(2)}, u32[]{:S(2)}) %all-to-all-start.2) | async-done | bytes 2097184 | tf_op jit(solution)/shard_map/all_to_all | solution.py:469
  131.6 3.8 %shard_map.135 = bf16[1040,1024]{1,0:T(8,128)(2,1)} custom-call(s32[16]{0:T(128)S(1)} %and_select_fusion.slot_ref, bf16[16,512,128]{2,1,0:T(8,128)(2,1)} %all-to-all-done.2.slab_ref, bf16[4,288,256]{2,1,0:T(8,128)(2,1)S(1)} %get-tuple-element.24.pick_ref, bf16[4,288,16]{2,1,0:T(8,128)(2,1)S(1)} %get-tuple-element.25.last_ref, ...), custom_call_target="tpu_custom_call" | custom-call | flops 603979776 | bytes 4194304 | tf_op jit(solution)/shard_map/pallas_call | solution.py:384
  (31 shorter events, 0.3 us)
Async XLA Ops:
  0.6 90.7 %copy-start = (bf16[1024,128]{1,0:T(8,128)(2,1)S(1)}, bf16[1024,128]{1,0:T(8,128)(2,1)}, u32[]{:S(2)}) copy-start(bf16[1024,128]{1,0:T(8,128)(2,1)} %param.17) | copy-start | bytes 786436
  2.1 14.9 %all-to-all-start = ((s32[16,1,16]{2,1,0:T(1,128)}), s32[16,1,16]{2,1,0:T(1,128)S(1)}, u32[]{:S(2)}, u32[]{:S(2)}) async-start(s32[16,1,16]{2,1,0:T(1,128)} %broadcast_in_dim.74), calls=%async_computation | async-start | bytes 16384 | tf_op jit(solution)/shard_map/all_to_all | solution.py:441
  17.0 0.6 copy-start.1
  21.0 6.9 %copy-start.6 = (s32[12]{0:T(128)S(1)}, s32[12]{0:T(128)}, u32[]{:S(2)}) copy-start(s32[12]{0:T(128)} %param.13) | copy-start | bytes 148
  21.0 57.6 %all-to-all-start.1 = ((bf16[16,528,128]{2,1,0:T(8,128)(2,1)}), bf16[16,528,128]{2,1,0:T(8,128)(2,1)S(1)}, u32[]{:S(2)}, u32[]{:S(2)}) async-start(bf16[16,528,128]{2,1,0:T(8,128)(2,1)} %shard_map.129), calls=%async_computation.1 | async-start | bytes 4325376 | tf_op jit(solution)/shard_map/all_to_all | solution.py:450
  38.0 5.9 %collective-permute-start = (f32[4,12,384]{2,1,0:T(8,128)}, f32[4,12,384]{2,1,0:T(8,128)S(1)}, u32[]{:S(2)}, u32[]{:S(2)}) collective-permute-start(f32[4,12,384]{2,1,0:T(8,128)} %shard_map.132), channel_id=1, source_target_pairs={{0,2},{2,0},{4,6},{6,4},{8,10},{10,8},{12,14},{14,12},{16,18},{18,... | collective-permute-start | bytes 221192 | tf_op jit(solution)/shard_map/ppermute | solution.py:466
  45.7 5.2 %collective-permute-start.1 = (f32[4,12,384]{2,1,0:T(8,128)S(1)}, f32[4,12,384]{2,1,0:T(8,128)S(1)}, u32[]{:S(2)}, u32[]{:S(2)}) collective-permute-start(f32[4,12,384]{2,1,0:T(8,128)S(1)} %add_select_fusion.3), channel_id=1, source_target_pairs={{0,4},{2,6},{4,0},{6,2},{8,12},{10,14},{12,8},{14,10},{16,20},{18,... | collective-permute-start | bytes 221192 | tf_op jit(solution)/shard_map/ppermute | solution.py:466
  51.1 14.1 %collective-permute-start.2 = (f32[4,12,384]{2,1,0:T(8,128)S(1)}, f32[4,12,384]{2,1,0:T(8,128)S(1)}, u32[]{:S(2)}, u32[]{:S(2)}) collective-permute-start(f32[4,12,384]{2,1,0:T(8,128)S(1)} %add_select_fusion.2), channel_id=1, source_target_pairs={{0,8},{2,10},{4,12},{6,14},{8,0},{10,2},{12,4},{14,6},{16,24},{18,... | collective-permute-start | bytes 221192 | tf_op jit(solution)/shard_map/ppermute | solution.py:466
  65.4 11.4 %collective-permute-start.3 = (bf16[4,12,384]{2,1,0:T(8,128)(2,1)S(1)}, bf16[4,12,384]{2,1,0:T(8,128)(2,1)S(1)}, u32[]{:S(2)}, u32[]{:S(2)}) collective-permute-start(bf16[4,12,384]{2,1,0:T(8,128)(2,1)S(1)} %fusion), channel_id=1, source_target_pairs={{0,16},{2,18},{4,20},{6,22},{8,24},{10,26},{12,28},{14,30},{16,0},... | collective-permute-start | bytes 110600 | tf_op jit(solution)/shard_map/ppermute | solution.py:464
  77.3 7.6 %copy-start.3 = (bf16[12,1024]{1,0:T(8,128)(2,1)S(1)}, bf16[12,1024]{1,0:T(8,128)(2,1)}, u32[]{:S(2)}) copy-start(bf16[12,1024]{1,0:T(8,128)(2,1)} %query_ref.1) | copy-start | bytes 73732
  77.3 7.6 %copy-start.4 = (bf16[12,1024]{1,0:T(8,128)(2,1)S(1)}, bf16[12,1024]{1,0:T(8,128)(2,1)}, u32[]{:S(2)}) copy-start(bf16[12,1024]{1,0:T(8,128)(2,1)} %param.15) | copy-start | bytes 73732
  77.4 7.8 %copy-start.5 = (bf16[12,1024]{1,0:T(8,128)(2,1)S(1)}, bf16[12,1024]{1,0:T(8,128)(2,1)}, u32[]{:S(2)}) copy-start(bf16[12,1024]{1,0:T(8,128)(2,1)} %param.16) | copy-start | bytes 73732
  77.4 7.9 %copy-start.7 = (u32[32]{0:T(128)S(1)}, u32[32]{0:T(128)}, u32[]{:S(2)}) copy-start(u32[32]{0:T(128)} %constant.64) | copy-start | bytes 388
  77.4 9.1 %copy-start.2 = (s32[16,1,16]{2,1,0:T(1,128)S(1)}, s32[16,1,16]{2,1,0:T(1,128)}, u32[]{:S(2)}) copy-start(s32[16,1,16]{2,1,0:T(1,128)} %copy-done.1) | copy-start | bytes 3076
  78.7 53.0 %all-to-all-start.2 = ((bf16[16,512,128]{2,1,0:T(8,128)(2,1)}), bf16[16,512,128]{2,1,0:T(8,128)(2,1)}, u32[]{:S(2)}, u32[]{:S(2)}) async-start(bf16[16,512,128]{2,1,0:T(8,128)(2,1)} %shard_map.134), calls=%async_computation.2 | async-start | bytes 4194304 | tf_op jit(solution)/shard_map/all_to_all | solution.py:469

commit v4 on v3

--- a/solution.py
+++ b/solution.py
@@ -15,6 +15,7 @@
 MOST_KEPT = BLOCK // 2
 LOW = -1e30
 VMEM_LIMIT = 56 * 1024 * 1024
+TURNS = 4
 VMEM_SMALL = 24 * 1024 * 1024
 
 
@@ -180,7 +181,6 @@
     peak = jnp.maximum(
         jnp.max(scores, axis=1, keepdims=True), jnp.max(fold_scores, axis=1, keepdims=True)
     )
-    peak = peak.astype(jnp.bfloat16).astype(jnp.float32)
     probs = jnp.where(member, jnp.exp(scores - peak), 0.0)
     fold_probs = jnp.where(fold_member, jnp.exp(fold_scores - peak), 0.0)
     total = jnp.sum(probs, axis=1, keepdims=True) + jnp.sum(fold_probs, axis=1, keepdims=True)
@@ -256,29 +256,35 @@
 
 
 def turn_kernel(geo, kept_ref, *refs):
-    main_ref, tail_refs = refs[0], refs[1:-6]
-    sent_ref, counts_ref, held_ref, counts_sem, in_sems, out_sems = refs[-6:]
+    main_ref, tail_refs = refs[0], refs[1:-7]
+    sent_ref, counts_ref, held_ref, counts_sem, main_sems, tail_sem, out_sems = refs[-7:]
+    me = lax.axis_index("seq")
+    peers, share = geo.peers, geo.share
     counts = pltpu.make_async_copy(kept_ref, counts_ref, counts_sem)
     counts.start()
-    me = lax.axis_index("seq")
-    peers, share = geo.peers, geo.share
-    arrivals = []
-    for p in range(peers):
-        held = held_ref.at[p]
-        copies = [pltpu.make_async_copy(main_ref.at[p], held.at[0:share], in_sems.at[0, p])]
-        for tail_ref in tail_refs:
-            tail = held.at[share : share + geo.tail]
-            copies.append(pltpu.make_async_copy(tail_ref.at[p], tail, in_sems.at[1, p]))
-        for copy in copies:
-            copy.start()
-        arrivals.append(copies)
+    tails = [
+        pltpu.make_async_copy(ref, held_ref.at[:, share : share + geo.tail], tail_sem)
+        for ref in tail_refs
+    ]
+    for copy in tails:
+        copy.start()
+    size = peers // TURNS
+    mains = []
+    for i in range(TURNS):
+        some = slice(i * size, (i + 1) * size)
+        mains.append(
+            pltpu.make_async_copy(main_ref.at[some], held_ref.at[some, 0:share], main_sems.at[i])
+        )
+        mains[i].start()
     counts.wait()
     start = my_start(counts_ref[...], me)
+    for copy in tails:
+        copy.wait()
     departures = []
     for p in range(peers):
+        if p % size == 0:
+            mains[p // size].wait()
         device = lax.rem(start + p, peers)
-        for copy in arrivals[p]:
-            copy.wait()
         departures.append(
             pltpu.make_async_copy(held_ref.at[p], sent_ref.at[device], out_sems.at[p])
         )
@@ -300,7 +306,8 @@
             pltpu.VMEM(kept.shape, jnp.int32),
             pltpu.VMEM(shape, jnp.bfloat16),
             pltpu.SemaphoreType.DMA,
-            pltpu.SemaphoreType.DMA((2, geo.peers)),
+            pltpu.SemaphoreType.DMA((TURNS,)),
+            pltpu.SemaphoreType.DMA,
             pltpu.SemaphoreType.DMA((geo.peers,)),
         ],
         compiler_params=pltpu.CompilerParams(vmem_limit_bytes=VMEM_LIMIT),
@@ -413,18 +420,25 @@
 
 
 def narrow(part):
+    peak, total = HD, HD + LANES // 2
     lane = lax.broadcasted_iota(jnp.int32, part.shape, len(part.shape) - 1)
-    high = part.astype(jnp.bfloat16)
-    low = (part - high.astype(jnp.float32)).astype(jnp.bfloat16)
-    return jnp.where(lane < HD + LANES * 3 // 4, high, low)
+    high = lax.reduce_precision(part, 8, 7)
+    rest = part - high
+    middle = lax.reduce_precision(rest, 8, 7)
+    low = lax.reduce_precision(rest - middle, 8, 7)
+    second = ((lane >= peak + 16) & (lane < peak + 32)) | (lane >= total + 16)
+    third = (lane >= peak + 32) & (lane < total)
+    return jnp.where(second, middle, jnp.where(third, low, high)).astype(jnp.bfloat16)
 
 
 def widen(part):
-    total = HD + LANES // 2
+    peak, total = HD, HD + LANES // 2
     part = part.astype(jnp.float32)
     lane = lax.broadcasted_iota(jnp.int32, part.shape, len(part.shape) - 1)
-    both = part[..., total : total + 1] + part[..., -1:]
-    return jnp.where(lane >= total, both, part)
+    peaks = part[..., peak : peak + 1] + part[..., peak + 16 : peak + 17]
+    peaks = peaks + part[..., peak + 32 : peak + 33]
+    totals = part[..., total : total + 1] + part[..., total + 16 : total + 17]
+    return jnp.where(lane >= total, totals, jnp.where(lane >= peak, peaks, part))
 
 
 def on_device(

time: 136 us -> 136 us (level)
  no operation moved by 1% of the time
where the time goes in v4:
time: 136 us; the launch traced here: 135 us
  waiting for transfers between devices  55.1 us (41%)
  Pallas kernels  37.5 us (28%)
  starting transfers between devices  25.5 us (19%)
  other arithmetic  8.1 us (6%)
  local copies, waits for them, and re-layouts  4.59 us (3%)
  blocking collectives  2.48 us (2%)
  between operations  1.6 us (1%)
    all_to_all x1, waiting for transfers between devices, on_device(): lax.all_to_all(sent, 'seq', split_axis=0, concat_axis=0, tiled=True)  32.7 us
    pallas_call x2, Pallas kernels, pack(): pl.pallas_call(functools.partial(pack_kernel, geo, bool(ends)), grid=(geo...  15.2 us
    ppermute x3, waiting for transfers between devices, on_device(): part = merge(part, lax.ppermute(part, 'seq', pairs))  13.1 us
    pallas_call x1, Pallas kernels, attend(): pl.pallas_call(functools.partial(attend_kernel, geo), grid=(geo.heads,),...  8.47 us
    ppermute x1, waiting for transfers between devices, on_device(): part = merge(part, widen(lax.ppermute(narrow(part), 'seq', pairs)))  7.96 us
    all_to_all x1, starting transfers between devices, on_device(): lax.all_to_all(jnp.broadcast_to(kept_count[None, :], (peers, block_count)...  7.17 us
    pallas_call x2, Pallas kernels, unpack(): pl.pallas_call(functools.partial(unpack_kernel, geo), grid=(geo.features...  7.12 us
    all_to_all x1, starting transfers between devices, on_device(): keys = lax.all_to_all(sent, 'seq', split_axis=0, concat_axis=0, tiled=True)  6.96 us
  transfers between devices with their start and end apart: 7, of which 6 were waited for; matrix products, arithmetic and copies ran while one was open for 8% of the time, Pallas kernels for 23%

profile of v4, /device:TPU:12, one launch (start us, length us, event | category | flops | bytes accessed | tf_op | source)
XLA Modules:
  0.0 134.9 jit_solution(17346759714592489543)
XLA Ops:
  0.6 0.0 copy-start
  0.6 0.8 bitcast_reduce_fusion
  1.5 0.6 broadcast_in_dim.81
  2.1 7.2 %all-to-all-start = ((s32[16,1,16]{2,1,0:T(1,128)}), s32[16,1,16]{2,1,0:T(1,128)S(1)}, u32[]{:S(2)}, u32[]{:S(2)}) async-start(s32[16,1,16]{2,1,0:T(1,128)} %broadcast_in_dim.81), calls=%async_computation | async-start | bytes 16384 | tf_op jit(solution)/shard_map/all_to_all | solution.py:455
  9.3 7.7 %shard_map.128 = (bf16[16,512,128]{2,1,0:T(8,128)(2,1)}, bf16[16,16,128]{2,1,0:T(8,128)(2,1)}) custom-call(s32[2048]{0:T(1024)} %keep_ref.3, s32[2048]{0:T(1024)} %weight_ref.3, bf16[2048,1024]{1,0:T(8,128)(2,1)} %key_ref.1, bf16[2048,1024]{1,0:T(8,128)(2,1)} %key_ref.1, bf16[2048,1024]{1,0:T(8,128)(2,1)} %cache_ref.3), custom_call_target="tpu_custom_call" | custom-call | flops 2348810240 | bytes 6291456 | tf_op jit(solution)/shard_map/pallas_call | solution.py:207
  17.0 0.0 copy-start.1
  17.0 0.6 copy-done.1
  17.6 2.9 %shard_map.129 = bf16[16,528,128]{2,1,0:T(8,128)(2,1)} custom-call(s32[16,16]{1,0:T(8,128)} %bitcast.34, bf16[16,512,128]{2,1,0:T(8,128)(2,1)} %get-tuple-element.20.refs_0_, bf16[16,16,128]{2,1,0:T(8,128)(2,1)} %get-tuple-element.21.refs_1_), custom_call_target="tpu_custom_call" | custom-call | bytes 4194304 | tf_op jit(solution)/shard_map/pallas_call | solution.py:300
  20.4 0.0 copy-start.6
  20.4 7.0 %all-to-all-start.1 = ((bf16[16,528,128]{2,1,0:T(8,128)(2,1)}), bf16[16,528,128]{2,1,0:T(8,128)(2,1)S(1)}, u32[]{:S(2)}, u32[]{:S(2)}) async-start(bf16[16,528,128]{2,1,0:T(8,128)(2,1)} %shard_map.129), calls=%async_computation.1 | async-start | bytes 4325376 | tf_op jit(solution)/shard_map/all_to_all | solution.py:464
  27.4 0.1 copy.28
  27.5 0.7 broadcast_subtract_fusion
  28.3 0.7 copy.29.first_ref
  29.0 8.5 %shard_map.132 = f32[4,12,384]{2,1,0:T(8,128)} custom-call(s32[2048]{0:T(1024)} %keep_ref.3, s32[2048]{0:T(1024)} %weight_ref.3, s32[12,1]{1,0:T(8,128)} %copy.29.first_ref, s32[12,1]{1,0:T(8,128)} %get-tuple-element.58.last_ref, bf16[12,1024]{1,0:T(8,128)(2,1)} %query_ref.1, bf16[2048,1024]{1,0:T(8,128)(2,1)} %key_ref.1, bf16[2048,1024]{1,0:T(8,128)(2,1)} %cache_ref.3), custom_call_target="tpu_custom_call" | custom-call | flops 201326592 | bytes 8388608 | tf_op jit(solution)/shard_map/pallas_call | solution.py:230
  37.4 1.5 %collective-permute-start = (f32[4,12,384]{2,1,0:T(8,128)}, f32[4,12,384]{2,1,0:T(8,128)S(1)}, u32[]{:S(2)}, u32[]{:S(2)}) collective-permute-start(f32[4,12,384]{2,1,0:T(8,128)} %shard_map.132), channel_id=1, source_target_pairs={{0,2},{2,0},{4,6},{6,4},{8,10},{10,8},{12,14},{14,12},{16,18},{18,... | collective-permute-start | bytes 221192 | tf_op jit(solution)/shard_map/ppermute | solution.py:480
  38.9 4.4 %collective-permute-done = f32[4,12,384]{2,1,0:T(8,128)S(1)} collective-permute-done((f32[4,12,384]{2,1,0:T(8,128)}, f32[4,12,384]{2,1,0:T(8,128)S(1)}, u32[]{:S(2)}, u32[]{:S(2)}) %collective-permute-start) | collective-permute-done | bytes 73760 | tf_op jit(solution)/shard_map/ppermute | solution.py:480
  43.3 0.9 fusion.17
  44.2 1.0 add_select_fusion.3
  45.2 0.1 collective-permute-start.1
  45.3 5.1 %collective-permute-done.1 = f32[4,12,384]{2,1,0:T(8,128)S(1)} collective-permute-done((f32[4,12,384]{2,1,0:T(8,128)S(1)}, f32[4,12,384]{2,1,0:T(8,128)S(1)}, u32[]{:S(2)}, u32[]{:S(2)}) %collective-permute-start.1) | collective-permute-done | bytes 73760 | tf_op jit(solution)/shard_map/ppermute | solution.py:480
  50.4 0.1 fusion.18
  50.5 0.1 add_select_fusion.2
  50.6 0.1 collective-permute-start.2
  50.7 7.6 %shard_map.133.refs_0_ = bf16[16,512,128]{2,1,0:T(8,128)(2,1)} custom-call(s32[2048]{0:T(1024)} %keep_ref.3, s32[2048]{0:T(1024)} %weight_ref.3, bf16[2048,1024]{1,0:T(8,128)(2,1)} %cache_ref.3), custom_call_target="tpu_custom_call" | custom-call | flops 2348810240 | bytes 6291456 | tf_op jit(solution)/shard_map/pallas_call | solution.py:207
  58.2 2.8 %shard_map.134 = bf16[16,512,128]{2,1,0:T(8,128)(2,1)} custom-call(s32[16,16]{1,0:T(8,128)} %bitcast.35, bf16[16,512,128]{2,1,0:T(8,128)(2,1)} %shard_map.133.refs_0_), custom_call_target="tpu_custom_call" | custom-call | bytes 4194304 | tf_op jit(solution)/shard_map/pallas_call | solution.py:300
  61.0 3.6 %collective-permute-done.2 = f32[4,12,384]{2,1,0:T(8,128)S(1)} collective-permute-done((f32[4,12,384]{2,1,0:T(8,128)S(1)}, f32[4,12,384]{2,1,0:T(8,128)S(1)}, u32[]{:S(2)}, u32[]{:S(2)}) %collective-permute-start.2) | collective-permute-done | bytes 73760 | tf_op jit(solution)/shard_map/ppermute | solution.py:480
  64.6 0.1 fusion.19
  64.8 0.1 add_select_fusion.1
  64.9 3.4 %collective-permute-start.3 = (bf16[4,12,384]{2,1,0:T(8,128)(2,1)S(1)}, bf16[4,12,384]{2,1,0:T(8,128)(2,1)S(1)}, u32[]{:S(2)}, u32[]{:S(2)}) collective-permute-start(bf16[4,12,384]{2,1,0:T(8,128)(2,1)S(1)} %fusion.1), channel_id=1, source_target_pairs={{0,16},{2,18},{4,20},{6,22},{8,24},{10,26},{12,28},{14,30},{16,0},... | collective-permute-start | bytes 110600 | tf_op jit(solution)/shard_map/ppermute | solution.py:478
  68.3 8.0 %collective-permute-done.3 = bf16[4,12,384]{2,1,0:T(8,128)(2,1)S(1)} collective-permute-done((bf16[4,12,384]{2,1,0:T(8,128)(2,1)S(1)}, bf16[4,12,384]{2,1,0:T(8,128)(2,1)S(1)}, u32[]{:S(2)}, u32[]{:S(2)}) %collective-permute-start.3) | collective-permute-done | bytes 36896 | tf_op jit(solution)/shard_map/ppermute | solution.py:478
  76.3 0.2 fusion.7
  76.5 0.1 select_select_fusion
  76.6 0.1 fusion.20
  76.7 0.1 add_select_fusion
  76.8 0.0 copy-start.3
  76.9 0.0 copy-start.7
  76.9 1.2 all-to-all-done.1.tail_ref.slab_ref
  78.1 6.3 %all-to-all-start.2 = ((bf16[16,512,128]{2,1,0:T(8,128)(2,1)}), bf16[16,512,128]{2,1,0:T(8,128)(2,1)}, u32[]{:S(2)}, u32[]{:S(2)}) async-start(bf16[16,512,128]{2,1,0:T(8,128)(2,1)} %shard_map.134), calls=%async_computation.2 | async-start | bytes 4194304 | tf_op jit(solution)/shard_map/all_to_all | solution.py:483
  84.5 0.1 fusion.5
  84.6 0.1 copy.38
  84.7 0.6 dynamic-slice
  86.0 0.1 broadcast_add_fusion
  86.1 0.1 copy.27
  86.2 0.1 reduce.1
  86.4 0.1 add.93
  86.4 0.3 reduce-window.27
  86.7 0.1 slice.71
  86.9 0.1 slice_reduce_fusion.2
  87.0 0.1 broadcast_add_fusion.1
  87.1 0.6 slice.73
  87.7 0.1 log.11
  87.7 0.4 convert_reduce_fusion
  88.1 0.1 convert_reduce_fusion.1
  88.2 1.0 select_reduce_fusion
  89.2 1.2 compare_select_fusion
  90.5 0.2 slice_reduce_fusion
  90.7 0.1 fusion.8
  90.9 0.2 fusion.23
  91.0 2.5 %all-reduce = bf16[12,128]{1,0:T(8,128)(2,1)S(1)} all-reduce(f32[12,128]{1,0:T(8,128)S(1)} %fusion.23), channel_id=2, replica_groups=mesh['seq'=16,'tp'=2] {'tp'}, use_global_device_ids=true, to_apply=%region_9.10.clone | all-reduce | flops 1536 | bytes 9216
  93.5 0.6 dynamic-slice_convert_fusion
  94.1 1.0 shard_map.130
  95.1 3.3 %shard_map.131 = bf16[1040,1024]{1,0:T(8,128)(2,1)} custom-call(s32[16]{0:T(128)S(1)} %and_select_fusion.slot_ref, bf16[16,528,128]{2,1,0:T(8,128)(2,1)S(1)} %all-to-all-done.1.tail_ref.slab_ref, bf16[4,288,256]{2,1,0:T(8,128)(2,1)S(1)} %get-tuple-element.24.pick_ref, bf16[4,288,16]{2,1,0:T(8,128)(2,1)S(1)} %get-tuple-element.25.last_ref, ...), custom_call_target="tpu_custom_call" | custom-call | flops 603979776 | bytes 4194304 | tf_op jit(solution)/shard_map/pallas_call | solution.py:391
  98.4 32.7 %all-to-all-done.2.slab_ref = bf16[16,512,128]{2,1,0:T(8,128)(2,1)} async-done(((bf16[16,512,128]{2,1,0:T(8,128)(2,1)}), bf16[16,512,128]{2,1,0:T(8,128)(2,1)}, u32[]{:S(2)}, u32[]{:S(2)}) %all-to-all-start.2) | async-done | bytes 2097184 | tf_op jit(solution)/shard_map/all_to_all | solution.py:483
  131.1 3.8 %shard_map.135 = bf16[1040,1024]{1,0:T(8,128)(2,1)} custom-call(s32[16]{0:T(128)S(1)} %and_select_fusion.slot_ref, bf16[16,512,128]{2,1,0:T(8,128)(2,1)} %all-to-all-done.2.slab_ref, bf16[4,288,256]{2,1,0:T(8,128)(2,1)S(1)} %get-tuple-element.24.pick_ref, bf16[4,288,16]{2,1,0:T(8,128)(2,1)S(1)} %get-tuple-element.25.last_ref, ...), custom_call_target="tpu_custom_call" | custom-call | flops 603979776 | bytes 4194304 | tf_op jit(solution)/shard_map/pallas_call | solution.py:391
  (31 shorter events, 0.4 us)
Async XLA Ops:
  0.6 90.2 %copy-start = (bf16[1024,128]{1,0:T(8,128)(2,1)S(1)}, bf16[1024,128]{1,0:T(8,128)(2,1)}, u32[]{:S(2)}) copy-start(bf16[1024,128]{1,0:T(8,128)(2,1)} %param.17) | copy-start | bytes 786436
  2.1 14.9 %all-to-all-start = ((s32[16,1,16]{2,1,0:T(1,128)}), s32[16,1,16]{2,1,0:T(1,128)S(1)}, u32[]{:S(2)}, u32[]{:S(2)}) async-start(s32[16,1,16]{2,1,0:T(1,128)} %broadcast_in_dim.81), calls=%async_computation | async-start | bytes 16384 | tf_op jit(solution)/shard_map/all_to_all | solution.py:455
  17.0 0.6 copy-start.1
  20.4 7.0 %copy-start.6 = (s32[12]{0:T(128)S(1)}, s32[12]{0:T(128)}, u32[]{:S(2)}) copy-start(s32[12]{0:T(128)} %param.13) | copy-start | bytes 148
  20.4 57.7 %all-to-all-start.1 = ((bf16[16,528,128]{2,1,0:T(8,128)(2,1)}), bf16[16,528,128]{2,1,0:T(8,128)(2,1)S(1)}, u32[]{:S(2)}, u32[]{:S(2)}) async-start(bf16[16,528,128]{2,1,0:T(8,128)(2,1)} %shard_map.129), calls=%async_computation.1 | async-start | bytes 4325376 | tf_op jit(solution)/shard_map/all_to_all | solution.py:464
  37.4 5.9 %collective-permute-start = (f32[4,12,384]{2,1,0:T(8,128)}, f32[4,12,384]{2,1,0:T(8,128)S(1)}, u32[]{:S(2)}, u32[]{:S(2)}) collective-permute-start(f32[4,12,384]{2,1,0:T(8,128)} %shard_map.132), channel_id=1, source_target_pairs={{0,2},{2,0},{4,6},{6,4},{8,10},{10,8},{12,14},{14,12},{16,18},{18,... | collective-permute-start | bytes 221192 | tf_op jit(solution)/shard_map/ppermute | solution.py:480
  45.2 5.2 %collective-permute-start.1 = (f32[4,12,384]{2,1,0:T(8,128)S(1)}, f32[4,12,384]{2,1,0:T(8,128)S(1)}, u32[]{:S(2)}, u32[]{:S(2)}) collective-permute-start(f32[4,12,384]{2,1,0:T(8,128)S(1)} %add_select_fusion.3), channel_id=1, source_target_pairs={{0,4},{2,6},{4,0},{6,2},{8,12},{10,14},{12,8},{14,10},{16,20},{18,... | collective-permute-start | bytes 221192 | tf_op jit(solution)/shard_map/ppermute | solution.py:480
  50.6 14.1 %collective-permute-start.2 = (f32[4,12,384]{2,1,0:T(8,128)S(1)}, f32[4,12,384]{2,1,0:T(8,128)S(1)}, u32[]{:S(2)}, u32[]{:S(2)}) collective-permute-start(f32[4,12,384]{2,1,0:T(8,128)S(1)} %add_select_fusion.2), channel_id=1, source_target_pairs={{0,8},{2,10},{4,12},{6,14},{8,0},{10,2},{12,4},{14,6},{16,24},{18,... | collective-permute-start | bytes 221192 | tf_op jit(solution)/shard_map/ppermute | solution.py:480
  64.9 11.4 %collective-permute-start.3 = (bf16[4,12,384]{2,1,0:T(8,128)(2,1)S(1)}, bf16[4,12,384]{2,1,0:T(8,128)(2,1)S(1)}, u32[]{:S(2)}, u32[]{:S(2)}) collective-permute-start(bf16[4,12,384]{2,1,0:T(8,128)(2,1)S(1)} %fusion.1), channel_id=1, source_target_pairs={{0,16},{2,18},{4,20},{6,22},{8,24},{10,26},{12,28},{14,30},{16,0},... | collective-permute-start | bytes 110600 | tf_op jit(solution)/shard_map/ppermute | solution.py:478
  76.8 7.6 %copy-start.3 = (bf16[12,1024]{1,0:T(8,128)(2,1)S(1)}, bf16[12,1024]{1,0:T(8,128)(2,1)}, u32[]{:S(2)}) copy-start(bf16[12,1024]{1,0:T(8,128)(2,1)} %query_ref.1) | copy-start | bytes 73732
  76.8 7.6 %copy-start.4 = (bf16[12,1024]{1,0:T(8,128)(2,1)S(1)}, bf16[12,1024]{1,0:T(8,128)(2,1)}, u32[]{:S(2)}) copy-start(bf16[12,1024]{1,0:T(8,128)(2,1)} %param.15) | copy-start | bytes 73732
  76.8 7.8 %copy-start.5 = (bf16[12,1024]{1,0:T(8,128)(2,1)S(1)}, bf16[12,1024]{1,0:T(8,128)(2,1)}, u32[]{:S(2)}) copy-start(bf16[12,1024]{1,0:T(8,128)(2,1)} %param.16) | copy-start | bytes 73732
  76.9 7.9 %copy-start.7 = (u32[32]{0:T(128)S(1)}, u32[32]{0:T(128)}, u32[]{:S(2)}) copy-start(u32[32]{0:T(128)} %constant.68) | copy-start | bytes 388
  76.9 9.1 %copy-start.2 = (s32[16,1,16]{2,1,0:T(1,128)S(1)}, s32[16,1,16]{2,1,0:T(1,128)}, u32[]{:S(2)}) copy-start(s32[16,1,16]{2,1,0:T(1,128)} %copy-done.1) | copy-start | bytes 3076
  78.1 53.0 %all-to-all-start.2 = ((bf16[16,512,128]{2,1,0:T(8,128)(2,1)}), bf16[16,512,128]{2,1,0:T(8,128)(2,1)}, u32[]{:S(2)}, u32[]{:S(2)}) async-start(bf16[16,512,128]{2,1,0:T(8,128)(2,1)} %shard_map.134), calls=%async_computation.2 | async-start | bytes 4194304 | tf_op jit(solution)/shard_map/all_to_all | solution.py:483

commit v5 on v4

--- a/solution.py
+++ b/solution.py
@@ -469,17 +469,16 @@
     part = attend(geo, keep_flags, drop_weight, first, last, queries, cache_keys, cache_values)
     (main,) = pack(geo, keep_flags, drop_weight, cache_values)
     sent = turn(geo, kept_all, main)
+    part = part.reshape(-1, part.shape[-1])
     distance = 1
-    while distance < peers:
-        if distance == peers // 2:
-            part, sent = lax.optimization_barrier((part, sent))
+    while distance < peers // 2:
         pairs = [(i, i ^ distance) for i in range(peers)]
-        if distance == peers // 2:
-            part = merge(part, widen(lax.ppermute(narrow(part), "seq", pairs)))
-        else:
-            part = merge(part, lax.ppermute(part, "seq", pairs))
+        part = merge(part, lax.ppermute(part, "seq", pairs))
         distance *= 2
     part, sent = lax.optimization_barrier((part, sent))
+    other = lax.ppermute(narrow(part), "seq", [(i, i ^ distance) for i in range(peers)])
+    other, sent = lax.optimization_barrier((other, sent))
+    part = merge(part, widen(other)).reshape(geo.heads, -1, part.shape[-1])
     values = lax.all_to_all(sent, "seq", split_axis=0, concat_axis=0, tiled=True)
 
     counts = jnp.sum(kept_all, axis=1) + block_count

time: 136 us -> 134 us (0.985)
  other arithmetic: 8.1 us -> 6.58 us
where the time goes in v5:
time: 134 us
  waiting for transfers between devices  55.2 us (41%)
  Pallas kernels  37.5 us (28%)
  starting transfers between devices  24.7 us (18%)
  other arithmetic  6.58 us (5%)
  local copies, waits for them, and re-layouts  5.5 us (4%)
  blocking collectives  2.48 us (2%)
  between operations  1.61 us (1%)
    all_to_all x1, waiting for transfers between devices, on_device(): lax.all_to_all(sent, 'seq', split_axis=0, concat_axis=0, tiled=True)  32.1 us
    pallas_call x2, Pallas kernels, pack(): pl.pallas_call(functools.partial(pack_kernel, geo, bool(ends)), grid=(geo...  15.2 us
    ppermute x3, waiting for transfers between devices, on_device(): part = merge(part, lax.ppermute(part, 'seq', pairs))  13.2 us
    pallas_call x1, Pallas kernels, attend(): pl.pallas_call(functools.partial(attend_kernel, geo), grid=(geo.heads,),...  8.47 us
    ppermute x1, waiting for transfers between devices, on_device(): lax.ppermute(narrow(part), 'seq', [(i, i ^ distance) for i in range(peers)])  7.91 us
    all_to_all x1, starting transfers between devices, on_device(): lax.all_to_all(jnp.broadcast_to(kept_count[None, :], (peers, block_count)...  7.17 us
    pallas_call x2, Pallas kernels, unpack(): pl.pallas_call(functools.partial(unpack_kernel, geo), grid=(geo.features...  7.09 us
    all_to_all x1, starting transfers between devices, on_device(): keys = lax.all_to_all(sent, 'seq', split_axis=0, concat_axis=0, tiled=True)  6.96 us
  transfers between devices with their start and end apart: 7, of which 6 were waited for; matrix products, arithmetic and copies ran while one was open for 8% of the time, Pallas kernels for 23%

profile of v5, /device:TPU:12, one launch (start us, length us, event | category | flops | bytes accessed | tf_op | source)
XLA Modules:
  0.0 133.7 jit_solution(4114217555370670480)
XLA Ops:
  0.6 0.0 copy-start
  0.6 0.8 bitcast_reduce_fusion
  1.5 0.6 broadcast_in_dim.81
  2.1 7.2 %all-to-all-start = ((s32[16,1,16]{2,1,0:T(1,128)}), s32[16,1,16]{2,1,0:T(1,128)S(1)}, u32[]{:S(2)}, u32[]{:S(2)}) async-start(s32[16,1,16]{2,1,0:T(1,128)} %broadcast_in_dim.81), calls=%async_computation | async-start | bytes 16384 | tf_op jit(solution)/shard_map/all_to_all | solution.py:455
  9.3 7.7 %shard_map.128 = (bf16[16,512,128]{2,1,0:T(8,128)(2,1)}, bf16[16,16,128]{2,1,0:T(8,128)(2,1)}) custom-call(s32[2048]{0:T(1024)} %keep_ref.3, s32[2048]{0:T(1024)} %weight_ref.3, bf16[2048,1024]{1,0:T(8,128)(2,1)} %key_ref.1, bf16[2048,1024]{1,0:T(8,128)(2,1)} %key_ref.1, bf16[2048,1024]{1,0:T(8,128)(2,1)} %cache_ref.3), custom_call_target="tpu_custom_call" | custom-call | flops 2348810240 | bytes 6291456 | tf_op jit(solution)/shard_map/pallas_call | solution.py:207
  17.0 0.6 copy-done.1
  17.6 2.9 %shard_map.129 = bf16[16,528,128]{2,1,0:T(8,128)(2,1)} custom-call(s32[16,16]{1,0:T(8,128)} %bitcast.32, bf16[16,512,128]{2,1,0:T(8,128)(2,1)} %get-tuple-element.20.refs_0_, bf16[16,16,128]{2,1,0:T(8,128)(2,1)} %get-tuple-element.21.refs_1_), custom_call_target="tpu_custom_call" | custom-call | bytes 4194304 | tf_op jit(solution)/shard_map/pallas_call | solution.py:300
  20.4 0.0 copy-start.6
  20.4 7.0 %all-to-all-start.1 = ((bf16[16,528,128]{2,1,0:T(8,128)(2,1)}), bf16[16,528,128]{2,1,0:T(8,128)(2,1)S(1)}, u32[]{:S(2)}, u32[]{:S(2)}) async-start(bf16[16,528,128]{2,1,0:T(8,128)(2,1)} %shard_map.129), calls=%async_computation.1 | async-start | bytes 4325376 | tf_op jit(solution)/shard_map/all_to_all | solution.py:464
  27.4 0.1 copy.36
  27.5 0.7 broadcast_subtract_fusion
  28.3 0.7 copy.37.first_ref
  29.0 8.5 %shard_map.132 = f32[4,12,384]{2,1,0:T(8,128)} custom-call(s32[2048]{0:T(1024)} %keep_ref.3, s32[2048]{0:T(1024)} %weight_ref.3, s32[12,1]{1,0:T(8,128)} %copy.37.first_ref, s32[12,1]{1,0:T(8,128)} %get-tuple-element.58.last_ref, bf16[12,1024]{1,0:T(8,128)(2,1)} %query_ref.1, bf16[2048,1024]{1,0:T(8,128)(2,1)} %key_ref.1, bf16[2048,1024]{1,0:T(8,128)(2,1)} %cache_ref.3), custom_call_target="tpu_custom_call" | custom-call | flops 201326592 | bytes 8388608 | tf_op jit(solution)/shard_map/pallas_call | solution.py:230
  37.4 0.9 reshape.142
  38.3 1.5 %collective-permute-start = (f32[48,384]{1,0:T(8,128)S(1)}, f32[48,384]{1,0:T(8,128)S(1)}, u32[]{:S(2)}, u32[]{:S(2)}) collective-permute-start(f32[48,384]{1,0:T(8,128)S(1)} %reshape.142), channel_id=1, source_target_pairs={{0,2},{2,0},{4,6},{6,4},{8,10},{10,8},{12,14},{14,12},{16,18},{18,... | collective-permute-start | bytes 221192 | tf_op jit(solution)/shard_map/ppermute | solution.py:476
  39.9 3.7 %collective-permute-done = f32[48,384]{1,0:T(8,128)S(1)} collective-permute-done((f32[48,384]{1,0:T(8,128)S(1)}, f32[48,384]{1,0:T(8,128)S(1)}, u32[]{:S(2)}, u32[]{:S(2)}) %collective-permute-start) | collective-permute-done | bytes 73760 | tf_op jit(solution)/shard_map/ppermute | solution.py:476
  43.5 0.1 fusion.17
  43.7 0.1 add_select_fusion.3
  43.8 0.1 collective-permute-start.1
  43.9 5.1 %collective-permute-done.1 = f32[48,384]{1,0:T(8,128)S(1)} collective-permute-done((f32[48,384]{1,0:T(8,128)S(1)}, f32[48,384]{1,0:T(8,128)S(1)}, u32[]{:S(2)}, u32[]{:S(2)}) %collective-permute-start.1) | collective-permute-done | bytes 73760 | tf_op jit(solution)/shard_map/ppermute | solution.py:476
  49.0 0.1 fusion.18
  49.1 0.1 add_select_fusion.2
  49.2 0.1 collective-permute-start.2
  49.3 7.6 %shard_map.133.refs_0_ = bf16[16,512,128]{2,1,0:T(8,128)(2,1)} custom-call(s32[2048]{0:T(1024)} %keep_ref.3, s32[2048]{0:T(1024)} %weight_ref.3, bf16[2048,1024]{1,0:T(8,128)(2,1)} %cache_ref.3), custom_call_target="tpu_custom_call" | custom-call | flops 2348810240 | bytes 6291456 | tf_op jit(solution)/shard_map/pallas_call | solution.py:207
  56.9 2.8 %shard_map.134 = bf16[16,512,128]{2,1,0:T(8,128)(2,1)} custom-call(s32[16,16]{1,0:T(8,128)} %bitcast.33, bf16[16,512,128]{2,1,0:T(8,128)(2,1)} %shard_map.133.refs_0_), custom_call_target="tpu_custom_call" | custom-call | bytes 4194304 | tf_op jit(solution)/shard_map/pallas_call | solution.py:300
  59.7 4.4 %collective-permute-done.2 = f32[48,384]{1,0:T(8,128)S(1)} collective-permute-done((f32[48,384]{1,0:T(8,128)S(1)}, f32[48,384]{1,0:T(8,128)S(1)}, u32[]{:S(2)}, u32[]{:S(2)}) %collective-permute-start.2) | collective-permute-done | bytes 73760 | tf_op jit(solution)/shard_map/ppermute | solution.py:476
  64.1 0.1 fusion.19
  64.3 0.1 add_select_fusion.1
  64.4 0.0 copy-start.3
  64.4 0.0 copy-start.7
  64.5 3.4 %collective-permute-start.3 = (bf16[48,384]{1,0:T(8,128)(2,1)S(1)}, bf16[48,384]{1,0:T(8,128)(2,1)S(1)}, u32[]{:S(2)}, u32[]{:S(2)}) collective-permute-start(bf16[48,384]{1,0:T(8,128)(2,1)S(1)} %fusion.1), channel_id=1, source_target_pairs={{0,16},{2,18},{4,20},{6,22},{8,24},{10,26},{12,28},{14,30},{16,0},... | collective-permute-start | bytes 110600 | tf_op jit(solution)/shard_map/ppermute | solution.py:479
  67.8 7.9 %collective-permute-done.3 = bf16[48,384]{1,0:T(8,128)(2,1)S(1)} collective-permute-done((bf16[48,384]{1,0:T(8,128)(2,1)S(1)}, bf16[48,384]{1,0:T(8,128)(2,1)S(1)}, u32[]{:S(2)}, u32[]{:S(2)}) %collective-permute-start.3) | collective-permute-done | bytes 36896 | tf_op jit(solution)/shard_map/ppermute | solution.py:479
  75.7 2.0 %all-to-all-done.1.tail_ref.slab_ref = bf16[16,528,128]{2,1,0:T(8,128)(2,1)S(1)} async-done(((bf16[16,528,128]{2,1,0:T(8,128)(2,1)}), bf16[16,528,128]{2,1,0:T(8,128)(2,1)S(1)}, u32[]{:S(2)}, u32[]{:S(2)}) %all-to-all-start.1) | async-done | bytes 2162720 | tf_op jit(solution)/shard_map/all_to_all | solution.py:464
  77.7 5.5 %all-to-all-start.2 = ((bf16[16,512,128]{2,1,0:T(8,128)(2,1)}), bf16[16,512,128]{2,1,0:T(8,128)(2,1)}, u32[]{:S(2)}, u32[]{:S(2)}) async-start(bf16[16,512,128]{2,1,0:T(8,128)(2,1)} %shard_map.134), calls=%async_computation.2 | async-start | bytes 4194304 | tf_op jit(solution)/shard_map/all_to_all | solution.py:482
  83.3 0.1 fusion.5
  83.4 0.1 copy.46
  83.6 0.6 dynamic-slice
  84.8 0.1 broadcast_add_fusion
  85.0 0.1 copy.35
  85.1 0.1 reduce.1
  85.2 0.1 add.89
  85.3 0.3 reduce-window.27
  85.6 0.1 slice.64
  85.7 0.1 slice_reduce_fusion.2
  85.8 0.1 broadcast_add_fusion.1
  85.9 0.6 slice.66
  86.5 0.1 log.11
  86.6 0.4 convert_reduce_fusion
  87.0 0.1 convert_reduce_fusion.1
  87.1 1.0 select_reduce_fusion
  88.1 1.2 compare_select_fusion
  89.3 0.2 fusion.8
  89.5 0.1 select_select_fusion
  89.6 0.1 fusion.20
  89.8 0.1 add_select_fusion
  89.9 0.2 slice_reduce_fusion
  90.1 0.1 fusion.6
  90.3 0.2 fusion.23
  90.4 2.5 %all-reduce = bf16[12,128]{1,0:T(8,128)(2,1)S(1)} all-reduce(f32[12,128]{1,0:T(8,128)S(1)} %fusion.23), channel_id=2, replica_groups=mesh['seq'=16,'tp'=2] {'tp'}, use_global_device_ids=true, to_apply=%region_9.10.clone | all-reduce | flops 1536 | bytes 9216
  92.9 0.6 dynamic-slice_convert_fusion
  93.5 1.0 shard_map.130
  94.5 3.3 %shard_map.131 = bf16[1040,1024]{1,0:T(8,128)(2,1)} custom-call(s32[16]{0:T(128)S(1)} %and_select_fusion.slot_ref, bf16[16,528,128]{2,1,0:T(8,128)(2,1)S(1)} %all-to-all-done.1.tail_ref.slab_ref, bf16[4,288,256]{2,1,0:T(8,128)(2,1)S(1)} %get-tuple-element.24.pick_ref, bf16[4,288,16]{2,1,0:T(8,128)(2,1)S(1)} %get-tuple-element.25.last_ref, ...), custom_call_target="tpu_custom_call" | custom-call | flops 603979776 | bytes 4194304 | tf_op jit(solution)/shard_map/pallas_call | solution.py:391
  97.8 32.1 %all-to-all-done.2.slab_ref = bf16[16,512,128]{2,1,0:T(8,128)(2,1)} async-done(((bf16[16,512,128]{2,1,0:T(8,128)(2,1)}), bf16[16,512,128]{2,1,0:T(8,128)(2,1)}, u32[]{:S(2)}, u32[]{:S(2)}) %all-to-all-start.2) | async-done | bytes 2097184 | tf_op jit(solution)/shard_map/all_to_all | solution.py:482
  129.9 3.8 %shard_map.135 = bf16[1040,1024]{1,0:T(8,128)(2,1)} custom-call(s32[16]{0:T(128)S(1)} %and_select_fusion.slot_ref, bf16[16,512,128]{2,1,0:T(8,128)(2,1)} %all-to-all-done.2.slab_ref, bf16[4,288,256]{2,1,0:T(8,128)(2,1)S(1)} %get-tuple-element.24.pick_ref, bf16[4,288,16]{2,1,0:T(8,128)(2,1)S(1)} %get-tuple-element.25.last_ref, ...), custom_call_target="tpu_custom_call" | custom-call | flops 603979776 | bytes 4194304 | tf_op jit(solution)/shard_map/pallas_call | solution.py:391
  (33 shorter events, 0.4 us)
Async XLA Ops:
  0.6 89.6 %copy-start = (bf16[1024,128]{1,0:T(8,128)(2,1)S(1)}, bf16[1024,128]{1,0:T(8,128)(2,1)}, u32[]{:S(2)}) copy-start(bf16[1024,128]{1,0:T(8,128)(2,1)} %param.17) | copy-start | bytes 786436
  2.1 14.9 %all-to-all-start = ((s32[16,1,16]{2,1,0:T(1,128)}), s32[16,1,16]{2,1,0:T(1,128)S(1)}, u32[]{:S(2)}, u32[]{:S(2)}) async-start(s32[16,1,16]{2,1,0:T(1,128)} %broadcast_in_dim.81), calls=%async_computation | async-start | bytes 16384 | tf_op jit(solution)/shard_map/all_to_all | solution.py:455
  17.0 0.6 copy-start.1
  20.4 7.0 %copy-start.6 = (s32[12]{0:T(128)S(1)}, s32[12]{0:T(128)}, u32[]{:S(2)}) copy-start(s32[12]{0:T(128)} %param.13) | copy-start | bytes 148
  20.4 57.3 %all-to-all-start.1 = ((bf16[16,528,128]{2,1,0:T(8,128)(2,1)}), bf16[16,528,128]{2,1,0:T(8,128)(2,1)S(1)}, u32[]{:S(2)}, u32[]{:S(2)}) async-start(bf16[16,528,128]{2,1,0:T(8,128)(2,1)} %shard_map.129), calls=%async_computation.1 | async-start | bytes 4325376 | tf_op jit(solution)/shard_map/all_to_all | solution.py:464
  38.3 5.2 %collective-permute-start = (f32[48,384]{1,0:T(8,128)S(1)}, f32[48,384]{1,0:T(8,128)S(1)}, u32[]{:S(2)}, u32[]{:S(2)}) collective-permute-start(f32[48,384]{1,0:T(8,128)S(1)} %reshape.142), channel_id=1, source_target_pairs={{0,2},{2,0},{4,6},{6,4},{8,10},{10,8},{12,14},{14,12},{16,18},{18,... | collective-permute-start | bytes 221192 | tf_op jit(solution)/shard_map/ppermute | solution.py:476
  43.8 5.2 %collective-permute-start.1 = (f32[48,384]{1,0:T(8,128)S(1)}, f32[48,384]{1,0:T(8,128)S(1)}, u32[]{:S(2)}, u32[]{:S(2)}) collective-permute-start(f32[48,384]{1,0:T(8,128)S(1)} %add_select_fusion.3), channel_id=1, source_target_pairs={{0,4},{2,6},{4,0},{6,2},{8,12},{10,14},{12,8},{14,10},{16,20},{18,... | collective-permute-start | bytes 221192 | tf_op jit(solution)/shard_map/ppermute | solution.py:476
  49.2 14.9 %collective-permute-start.2 = (f32[48,384]{1,0:T(8,128)S(1)}, f32[48,384]{1,0:T(8,128)S(1)}, u32[]{:S(2)}, u32[]{:S(2)}) collective-permute-start(f32[48,384]{1,0:T(8,128)S(1)} %add_select_fusion.2), channel_id=1, source_target_pairs={{0,8},{2,10},{4,12},{6,14},{8,0},{10,2},{12,4},{14,6},{16,24},{18,... | collective-permute-start | bytes 221192 | tf_op jit(solution)/shard_map/ppermute | solution.py:476
  64.4 18.9 %copy-start.3 = (bf16[12,1024]{1,0:T(8,128)(2,1)S(1)}, bf16[12,1024]{1,0:T(8,128)(2,1)}, u32[]{:S(2)}) copy-start(bf16[12,1024]{1,0:T(8,128)(2,1)} %query_ref.1) | copy-start | bytes 73732
  64.4 18.9 %copy-start.4 = (bf16[12,1024]{1,0:T(8,128)(2,1)S(1)}, bf16[12,1024]{1,0:T(8,128)(2,1)}, u32[]{:S(2)}) copy-start(bf16[12,1024]{1,0:T(8,128)(2,1)} %param.15) | copy-start | bytes 73732
  64.4 19.1 %copy-start.5 = (bf16[12,1024]{1,0:T(8,128)(2,1)S(1)}, bf16[12,1024]{1,0:T(8,128)(2,1)}, u32[]{:S(2)}) copy-start(bf16[12,1024]{1,0:T(8,128)(2,1)} %param.16) | copy-start | bytes 73732
  64.4 19.1 %copy-start.7 = (u32[32]{0:T(128)S(1)}, u32[32]{0:T(128)}, u32[]{:S(2)}) copy-start(u32[32]{0:T(128)} %constant.68) | copy-start | bytes 388
  64.4 20.4 %copy-start.2 = (s32[16,1,16]{2,1,0:T(1,128)S(1)}, s32[16,1,16]{2,1,0:T(1,128)}, u32[]{:S(2)}) copy-start(s32[16,1,16]{2,1,0:T(1,128)} %copy-done.1) | copy-start | bytes 3076
  64.5 11.3 %collective-permute-start.3 = (bf16[48,384]{1,0:T(8,128)(2,1)S(1)}, bf16[48,384]{1,0:T(8,128)(2,1)S(1)}, u32[]{:S(2)}, u32[]{:S(2)}) collective-permute-start(bf16[48,384]{1,0:T(8,128)(2,1)S(1)} %fusion.1), channel_id=1, source_target_pairs={{0,16},{2,18},{4,20},{6,22},{8,24},{10,26},{12,28},{14,30},{16,0},... | collective-permute-start | bytes 110600 | tf_op jit(solution)/shard_map/ppermute | solution.py:479
  77.7 52.2 %all-to-all-start.2 = ((bf16[16,512,128]{2,1,0:T(8,128)(2,1)}), bf16[16,512,128]{2,1,0:T(8,128)(2,1)}, u32[]{:S(2)}, u32[]{:S(2)}) async-start(bf16[16,512,128]{2,1,0:T(8,128)(2,1)} %shard_map.134), calls=%async_computation.2 | async-start | bytes 4194304 | tf_op jit(solution)/shard_map/all_to_all | solution.py:482

commit v6 on v5

--- a/solution.py
+++ b/solution.py
@@ -476,9 +476,18 @@
         part = merge(part, lax.ppermute(part, "seq", pairs))
         distance *= 2
     part, sent = lax.optimization_barrier((part, sent))
+    quarter = part.shape[0] // 4
+    part = lax.dynamic_slice_in_dim(part, me % 4 * quarter, quarter, 0)
     other = lax.ppermute(narrow(part), "seq", [(i, i ^ distance) for i in range(peers)])
     other, sent = lax.optimization_barrier((other, sent))
-    part = merge(part, widen(other)).reshape(geo.heads, -1, part.shape[-1])
+    part = merge(part, widen(other))
+    for distance in (1, 2):
+        other = lax.ppermute(part, "seq", [(i, i ^ distance) for i in range(peers)])
+        is_low = me & distance == 0
+        part = jnp.concatenate(
+            [jnp.where(is_low, part, other), jnp.where(is_low, other, part)], axis=0
+        )
+    part = part.reshape(geo.heads, -1, part.shape[-1])
     values = lax.all_to_all(sent, "seq", split_axis=0, concat_axis=0, tiled=True)
 
     counts = jnp.sum(kept_all, axis=1) + block_count

time: 134 us -> 134 us (level)
  waiting for transfers between devices: 55.2 us -> 52.5 us
  starting transfers between devices: 24.7 us -> 26.3 us
    all_to_all x1, waiting for transfers between devices: 32.1 us -> 26.9 us  [on_device(): lax.all_to_all(sent, 'seq', split_axis=0, concat_axis=0, tiled=True)]
    ppermute x0 -> x2, waiting for transfers between devices: none -> 4.67 us  [on_device(): other = lax.ppermute(part, 'seq', [(i, i ^ distance) for i in range(peers)])]
    ppermute x0 -> x2, starting transfers between devices: none -> 2.16 us  [on_device(): other = lax.ppermute(part, 'seq', [(i, i ^ distance) for i in range(peers)])]
    ppermute x3, waiting for transfers between devices: 13.2 us -> 11.6 us  [on_device(): part = merge(part, lax.ppermute(part, 'seq', pairs))]
  transfers between devices with their start and end apart: 7 -> 9, of which waited for: 6 -> 8; matrix products, arithmetic and copies ran while one was open for 8% -> 8% of each run, Pallas kernels for 23% -> 23%
where the time goes in v6:
time: 134 us; the launch traced here: 133 us
  waiting for transfers between devices  52.5 us (39%)
  Pallas kernels  37.6 us (28%)
  starting transfers between devices  26.3 us (20%)
  other arithmetic  6.64 us (5%)
  local copies, waits for them, and re-layouts  5.49 us (4%)
  blocking collectives  2.48 us (2%)
  between operations  1.61 us (1%)
    all_to_all x1, waiting for transfers between devices, on_device(): lax.all_to_all(sent, 'seq', split_axis=0, concat_axis=0, tiled=True)  26.9 us
    pallas_call x2, Pallas kernels, pack(): pl.pallas_call(functools.partial(pack_kernel, geo, bool(ends)), grid=(geo...  15.2 us
    ppermute x3, waiting for transfers between devices, on_device(): part = merge(part, lax.ppermute(part, 'seq', pairs))  11.6 us
    pallas_call x1, Pallas kernels, attend(): pl.pallas_call(functools.partial(attend_kernel, geo), grid=(geo.heads,),...  8.47 us
    all_to_all x1, starting transfers between devices, on_device(): lax.all_to_all(jnp.broadcast_to(kept_count[None, :], (peers, block_count)...  7.17 us
    pallas_call x2, Pallas kernels, unpack(): pl.pallas_call(functools.partial(unpack_kernel, geo), grid=(geo.features...  7.11 us
    ppermute x1, waiting for transfers between devices, on_device(): lax.ppermute(narrow(part), 'seq', [(i, i ^ distance) for i in range(peers)])  7.09 us
    all_to_all x1, starting transfers between devices, on_device(): keys = lax.all_to_all(sent, 'seq', split_axis=0, concat_axis=0, tiled=True)  7.06 us
  transfers between devices with their start and end apart: 9, of which 8 were waited for; matrix products, arithmetic and copies ran while one was open for 8% of the time, Pallas kernels for 23%

profile of v6, /device:TPU:12, one launch (start us, length us, event | category | flops | bytes accessed | tf_op | source)
XLA Modules:
  0.0 132.8 jit_solution(2723905742944577499)
XLA Ops:
  0.6 0.8 bitcast_reduce_fusion
  1.5 0.6 broadcast_in_dim.84
  2.1 7.2 %all-to-all-start = ((s32[16,1,16]{2,1,0:T(1,128)}), s32[16,1,16]{2,1,0:T(1,128)S(1)}, u32[]{:S(2)}, u32[]{:S(2)}) async-start(s32[16,1,16]{2,1,0:T(1,128)} %broadcast_in_dim.84), calls=%async_computation | async-start | bytes 16384 | tf_op jit(solution)/shard_map/all_to_all | solution.py:455
  9.3 7.7 %shard_map.128 = (bf16[16,512,128]{2,1,0:T(8,128)(2,1)}, bf16[16,16,128]{2,1,0:T(8,128)(2,1)}) custom-call(s32[2048]{0:T(1024)} %keep_ref.3, s32[2048]{0:T(1024)} %weight_ref.3, bf16[2048,1024]{1,0:T(8,128)(2,1)} %key_ref.1, bf16[2048,1024]{1,0:T(8,128)(2,1)} %key_ref.1, bf16[2048,1024]{1,0:T(8,128)(2,1)} %cache_ref.3), custom_call_target="tpu_custom_call" | custom-call | flops 2348810240 | bytes 6291456 | tf_op jit(solution)/shard_map/pallas_call | solution.py:207
  17.0 0.6 copy-done.1
  17.6 2.9 %shard_map.129 = bf16[16,528,128]{2,1,0:T(8,128)(2,1)} custom-call(s32[16,16]{1,0:T(8,128)} %bitcast.32, bf16[16,512,128]{2,1,0:T(8,128)(2,1)} %get-tuple-element.20.refs_0_, bf16[16,16,128]{2,1,0:T(8,128)(2,1)} %get-tuple-element.21.refs_1_), custom_call_target="tpu_custom_call" | custom-call | bytes 4194304 | tf_op jit(solution)/shard_map/pallas_call | solution.py:300
  20.5 7.1 %all-to-all-start.1 = ((bf16[16,528,128]{2,1,0:T(8,128)(2,1)}), bf16[16,528,128]{2,1,0:T(8,128)(2,1)S(1)}, u32[]{:S(2)}, u32[]{:S(2)}) async-start(bf16[16,528,128]{2,1,0:T(8,128)(2,1)} %shard_map.129), calls=%async_computation.1 | async-start | bytes 4325376 | tf_op jit(solution)/shard_map/all_to_all | solution.py:464
  27.7 0.1 fusion.3
  27.8 0.1 copy.46
  27.9 0.6 dynamic-slice
  29.2 0.1 copy.36
  29.3 0.7 broadcast_subtract_fusion
  30.0 0.7 copy.37.first_ref
  30.7 8.5 %shard_map.132 = f32[4,12,384]{2,1,0:T(8,128)} custom-call(s32[2048]{0:T(1024)} %keep_ref.3, s32[2048]{0:T(1024)} %weight_ref.3, s32[12,1]{1,0:T(8,128)} %copy.37.first_ref, s32[12,1]{1,0:T(8,128)} %get-tuple-element.62.last_ref, bf16[12,1024]{1,0:T(8,128)(2,1)} %query_ref.1, bf16[2048,1024]{1,0:T(8,128)(2,1)} %key_ref.1, bf16[2048,1024]{1,0:T(8,128)(2,1)} %cache_ref.3), custom_call_target="tpu_custom_call" | custom-call | flops 201326592 | bytes 8388608 | tf_op jit(solution)/shard_map/pallas_call | solution.py:230
  39.2 0.9 reshape.142
  40.1 1.5 %collective-permute-start = (f32[48,384]{1,0:T(8,128)S(1)}, f32[48,384]{1,0:T(8,128)S(1)}, u32[]{:S(2)}, u32[]{:S(2)}) collective-permute-start(f32[48,384]{1,0:T(8,128)S(1)} %reshape.142), channel_id=1, source_target_pairs={{0,2},{2,0},{4,6},{6,4},{8,10},{10,8},{12,14},{14,12},{16,18},{18,... | collective-permute-start | bytes 221192 | tf_op jit(solution)/shard_map/ppermute | solution.py:476
  41.6 4.2 %collective-permute-done = f32[48,384]{1,0:T(8,128)S(1)} collective-permute-done((f32[48,384]{1,0:T(8,128)S(1)}, f32[48,384]{1,0:T(8,128)S(1)}, u32[]{:S(2)}, u32[]{:S(2)}) %collective-permute-start) | collective-permute-done | bytes 73760 | tf_op jit(solution)/shard_map/ppermute | solution.py:476
  45.8 0.1 fusion.17
  45.9 0.1 add_select_fusion.2
  46.0 0.1 collective-permute-start.1
  46.1 4.5 %collective-permute-done.1 = f32[48,384]{1,0:T(8,128)S(1)} collective-permute-done((f32[48,384]{1,0:T(8,128)S(1)}, f32[48,384]{1,0:T(8,128)S(1)}, u32[]{:S(2)}, u32[]{:S(2)}) %collective-permute-start.1) | collective-permute-done | bytes 73760 | tf_op jit(solution)/shard_map/ppermute | solution.py:476
  50.6 0.1 fusion.18
  50.8 0.1 add_select_fusion.1
  50.9 0.1 collective-permute-start.2
  50.9 7.6 %shard_map.133.refs_0_ = bf16[16,512,128]{2,1,0:T(8,128)(2,1)} custom-call(s32[2048]{0:T(1024)} %keep_ref.3, s32[2048]{0:T(1024)} %weight_ref.3, bf16[2048,1024]{1,0:T(8,128)(2,1)} %cache_ref.3), custom_call_target="tpu_custom_call" | custom-call | flops 2348810240 | bytes 6291456 | tf_op jit(solution)/shard_map/pallas_call | solution.py:207
  58.5 2.9 %shard_map.134 = bf16[16,512,128]{2,1,0:T(8,128)(2,1)} custom-call(s32[16,16]{1,0:T(8,128)} %bitcast.33, bf16[16,512,128]{2,1,0:T(8,128)(2,1)} %shard_map.133.refs_0_), custom_call_target="tpu_custom_call" | custom-call | bytes 4194304 | tf_op jit(solution)/shard_map/pallas_call | solution.py:300
  61.4 2.9 %collective-permute-done.2 = f32[48,384]{1,0:T(8,128)S(1)} collective-permute-done((f32[48,384]{1,0:T(8,128)S(1)}, f32[48,384]{1,0:T(8,128)S(1)}, u32[]{:S(2)}, u32[]{:S(2)}) %collective-permute-start.2) | collective-permute-done | bytes 73760 | tf_op jit(solution)/shard_map/ppermute | solution.py:476
  64.3 0.1 fusion.19
  64.5 0.1 add_select_fusion
  64.6 3.0 %collective-permute-start.3 = (bf16[12,384]{1,0:T(8,128)(2,1)S(1)}, bf16[12,384]{1,0:T(8,128)(2,1)S(1)}, u32[]{:S(2)}, u32[]{:S(2)}) collective-permute-start(bf16[12,384]{1,0:T(8,128)(2,1)S(1)} %fusion.6), channel_id=1, source_target_pairs={{0,16},{2,18},{4,20},{6,22},{8,24},{10,26},{12,28},{14,30},{16,0},... | collective-permute-start | bytes 27656 | tf_op jit(solution)/shard_map/ppermute | solution.py:481
  67.6 0.1 broadcast_add_fusion
  67.7 7.1 %collective-permute-done.3 = bf16[12,384]{1,0:T(8,128)(2,1)S(1)} collective-permute-done((bf16[12,384]{1,0:T(8,128)(2,1)S(1)}, bf16[12,384]{1,0:T(8,128)(2,1)S(1)}, u32[]{:S(2)}, u32[]{:S(2)}) %collective-permute-start.3) | collective-permute-done | bytes 9248 | tf_op jit(solution)/shard_map/ppermute | solution.py:481
  74.8 2.3 %all-to-all-done.1.tail_ref.slab_ref = bf16[16,528,128]{2,1,0:T(8,128)(2,1)S(1)} async-done(((bf16[16,528,128]{2,1,0:T(8,128)(2,1)}), bf16[16,528,128]{2,1,0:T(8,128)(2,1)S(1)}, u32[]{:S(2)}, u32[]{:S(2)}) %all-to-all-start.1) | async-done | bytes 2162720 | tf_op jit(solution)/shard_map/all_to_all | solution.py:464
  77.1 5.3 %all-to-all-start.2 = ((bf16[16,512,128]{2,1,0:T(8,128)(2,1)}), bf16[16,512,128]{2,1,0:T(8,128)(2,1)}, u32[]{:S(2)}, u32[]{:S(2)}) async-start(bf16[16,512,128]{2,1,0:T(8,128)(2,1)} %shard_map.134), calls=%async_computation.2 | async-start | bytes 4194304 | tf_op jit(solution)/shard_map/all_to_all | solution.py:491
  82.4 0.1 copy.35
  82.5 0.1 reduce.1
  82.6 0.1 add.98
  82.7 0.3 reduce-window.27
  83.0 0.1 slice.64
  83.1 0.1 slice_reduce_fusion.2
  83.2 0.1 broadcast_add_fusion.1
  83.3 0.6 slice.66
  83.9 0.4 convert_reduce_fusion
  84.3 0.1 convert_reduce_fusion.1
  84.4 1.3 compare_select_fusion
  85.7 0.2 fusion.8
  85.9 0.1 select_select_fusion
  85.9 0.2 fusion.20
  86.2 0.1 add_select_fusion.3
  86.3 1.5 %collective-permute-start.4 = (f32[12,384]{1,0:T(8,128)S(1)}, f32[12,384]{1,0:T(8,128)S(1)}, u32[]{:S(2)}, u32[]{:S(2)}) collective-permute-start(f32[12,384]{1,0:T(8,128)S(1)} %add_select_fusion.3), channel_id=1, source_target_pairs={{0,2},{2,0},{4,6},{6,4},{8,10},{10,8},{12,14},{14,12},{16,18},{18,... | collective-permute-start | bytes 55304 | tf_op jit(solution)/shard_map/ppermute | solution.py:485
  87.8 0.1 log.11
  87.9 2.3 %collective-permute-done.4 = f32[12,384]{1,0:T(8,128)S(1)} collective-permute-done((f32[12,384]{1,0:T(8,128)S(1)}, f32[12,384]{1,0:T(8,128)S(1)}, u32[]{:S(2)}, u32[]{:S(2)}) %collective-permute-start.4) | collective-permute-done | bytes 18464 | tf_op jit(solution)/shard_map/ppermute | solution.py:485
  90.2 0.6 collective-permute-start.5
  90.8 1.0 select_reduce_fusion
  91.8 2.4 %collective-permute-done.5 = f32[24,384]{1,0:T(8,128)S(1)} collective-permute-done((f32[24,384]{1,0:T(8,128)S(1)}, f32[24,384]{1,0:T(8,128)S(1)}, u32[]{:S(2)}, u32[]{:S(2)}) %collective-permute-start.5) | collective-permute-done | bytes 36896 | tf_op jit(solution)/shard_map/ppermute | solution.py:485
  94.2 0.2 slice_reduce_fusion
  94.4 0.1 fusion.4
  94.6 0.2 fusion.23
  94.8 2.5 %all-reduce = bf16[12,128]{1,0:T(8,128)(2,1)S(1)} all-reduce(f32[12,128]{1,0:T(8,128)S(1)} %fusion.23), channel_id=2, replica_groups=mesh['seq'=16,'tp'=2] {'tp'}, use_global_device_ids=true, to_apply=%region_9.10.clone | all-reduce | flops 1536 | bytes 9216
  97.2 0.6 dynamic-slice_convert_fusion
  97.8 1.0 shard_map.130
  98.8 3.3 %shard_map.131 = bf16[1040,1024]{1,0:T(8,128)(2,1)} custom-call(s32[16]{0:T(128)S(1)} %and_select_fusion.slot_ref, bf16[16,528,128]{2,1,0:T(8,128)(2,1)S(1)} %all-to-all-done.1.tail_ref.slab_ref, bf16[4,288,256]{2,1,0:T(8,128)(2,1)S(1)} %get-tuple-element.24.pick_ref, bf16[4,288,16]{2,1,0:T(8,128)(2,1)S(1)} %get-tuple-element.25.last_ref, ...), custom_call_target="tpu_custom_call" | custom-call | flops 603979776 | bytes 4194304 | tf_op jit(solution)/shard_map/pallas_call | solution.py:391
  102.1 26.9 %all-to-all-done.2.slab_ref = bf16[16,512,128]{2,1,0:T(8,128)(2,1)} async-done(((bf16[16,512,128]{2,1,0:T(8,128)(2,1)}), bf16[16,512,128]{2,1,0:T(8,128)(2,1)}, u32[]{:S(2)}, u32[]{:S(2)}) %all-to-all-start.2) | async-done | bytes 2097184 | tf_op jit(solution)/shard_map/all_to_all | solution.py:491
  129.1 3.8 %shard_map.135 = bf16[1040,1024]{1,0:T(8,128)(2,1)} custom-call(s32[16]{0:T(128)S(1)} %and_select_fusion.slot_ref, bf16[16,512,128]{2,1,0:T(8,128)(2,1)} %all-to-all-done.2.slab_ref, bf16[4,288,256]{2,1,0:T(8,128)(2,1)S(1)} %get-tuple-element.24.pick_ref, bf16[4,288,16]{2,1,0:T(8,128)(2,1)S(1)} %get-tuple-element.25.last_ref, ...), custom_call_target="tpu_custom_call" | custom-call | flops 603979776 | bytes 4194304 | tf_op jit(solution)/shard_map/pallas_call | solution.py:391
  (41 shorter events, 0.4 us)
Async XLA Ops:
  0.6 94.0 %copy-start = (bf16[1024,128]{1,0:T(8,128)(2,1)S(1)}, bf16[1024,128]{1,0:T(8,128)(2,1)}, u32[]{:S(2)}) copy-start(bf16[1024,128]{1,0:T(8,128)(2,1)} %param.17) | copy-start | bytes 786436
  2.1 14.9 %all-to-all-start = ((s32[16,1,16]{2,1,0:T(1,128)}), s32[16,1,16]{2,1,0:T(1,128)S(1)}, u32[]{:S(2)}, u32[]{:S(2)}) async-start(s32[16,1,16]{2,1,0:T(1,128)} %broadcast_in_dim.84), calls=%async_computation | async-start | bytes 16384 | tf_op jit(solution)/shard_map/all_to_all | solution.py:455
  17.0 0.6 copy-start.1
  20.5 7.1 %copy-start.3 = (bf16[12,1024]{1,0:T(8,128)(2,1)S(1)}, bf16[12,1024]{1,0:T(8,128)(2,1)}, u32[]{:S(2)}) copy-start(bf16[12,1024]{1,0:T(8,128)(2,1)} %query_ref.1) | copy-start | bytes 73732
  20.5 7.1 %copy-start.4 = (bf16[12,1024]{1,0:T(8,128)(2,1)S(1)}, bf16[12,1024]{1,0:T(8,128)(2,1)}, u32[]{:S(2)}) copy-start(bf16[12,1024]{1,0:T(8,128)(2,1)} %param.15) | copy-start | bytes 73732
  20.5 7.4 %copy-start.5 = (bf16[12,1024]{1,0:T(8,128)(2,1)S(1)}, bf16[12,1024]{1,0:T(8,128)(2,1)}, u32[]{:S(2)}) copy-start(bf16[12,1024]{1,0:T(8,128)(2,1)} %param.16) | copy-start | bytes 73732
  20.5 7.4 %copy-start.7 = (u32[32]{0:T(128)S(1)}, u32[32]{0:T(128)}, u32[]{:S(2)}) copy-start(u32[32]{0:T(128)} %constant.88) | copy-start | bytes 388
  20.5 8.7 %copy-start.6 = (s32[12]{0:T(128)S(1)}, s32[12]{0:T(128)}, u32[]{:S(2)}) copy-start(s32[12]{0:T(128)} %param.13) | copy-start | bytes 148
  20.5 56.6 %all-to-all-start.1 = ((bf16[16,528,128]{2,1,0:T(8,128)(2,1)}), bf16[16,528,128]{2,1,0:T(8,128)(2,1)S(1)}, u32[]{:S(2)}, u32[]{:S(2)}) async-start(bf16[16,528,128]{2,1,0:T(8,128)(2,1)} %shard_map.129), calls=%async_computation.1 | async-start | bytes 4325376 | tf_op jit(solution)/shard_map/all_to_all | solution.py:464
  40.1 5.7 %collective-permute-start = (f32[48,384]{1,0:T(8,128)S(1)}, f32[48,384]{1,0:T(8,128)S(1)}, u32[]{:S(2)}, u32[]{:S(2)}) collective-permute-start(f32[48,384]{1,0:T(8,128)S(1)} %reshape.142), channel_id=1, source_target_pairs={{0,2},{2,0},{4,6},{6,4},{8,10},{10,8},{12,14},{14,12},{16,18},{18,... | collective-permute-start | bytes 221192 | tf_op jit(solution)/shard_map/ppermute | solution.py:476
  46.0 4.6 %collective-permute-start.1 = (f32[48,384]{1,0:T(8,128)S(1)}, f32[48,384]{1,0:T(8,128)S(1)}, u32[]{:S(2)}, u32[]{:S(2)}) collective-permute-start(f32[48,384]{1,0:T(8,128)S(1)} %add_select_fusion.2), channel_id=1, source_target_pairs={{0,4},{2,6},{4,0},{6,2},{8,12},{10,14},{12,8},{14,10},{16,20},{18,... | collective-permute-start | bytes 221192 | tf_op jit(solution)/shard_map/ppermute | solution.py:476
  50.9 13.5 %collective-permute-start.2 = (f32[48,384]{1,0:T(8,128)S(1)}, f32[48,384]{1,0:T(8,128)S(1)}, u32[]{:S(2)}, u32[]{:S(2)}) collective-permute-start(f32[48,384]{1,0:T(8,128)S(1)} %add_select_fusion.1), channel_id=1, source_target_pairs={{0,8},{2,10},{4,12},{6,14},{8,0},{10,2},{12,4},{14,6},{16,24},{18,... | collective-permute-start | bytes 221192 | tf_op jit(solution)/shard_map/ppermute | solution.py:476
  58.5 9.1 %copy-start.2 = (s32[16,1,16]{2,1,0:T(1,128)S(1)}, s32[16,1,16]{2,1,0:T(1,128)}, u32[]{:S(2)}) copy-start(s32[16,1,16]{2,1,0:T(1,128)} %copy-done.1) | copy-start | bytes 3076
  64.6 10.2 %collective-permute-start.3 = (bf16[12,384]{1,0:T(8,128)(2,1)S(1)}, bf16[12,384]{1,0:T(8,128)(2,1)S(1)}, u32[]{:S(2)}, u32[]{:S(2)}) collective-permute-start(bf16[12,384]{1,0:T(8,128)(2,1)S(1)} %fusion.6), channel_id=1, source_target_pairs={{0,16},{2,18},{4,20},{6,22},{8,24},{10,26},{12,28},{14,30},{16,0},... | collective-permute-start | bytes 27656 | tf_op jit(solution)/shard_map/ppermute | solution.py:481
  77.1 52.0 %all-to-all-start.2 = ((bf16[16,512,128]{2,1,0:T(8,128)(2,1)}), bf16[16,512,128]{2,1,0:T(8,128)(2,1)}, u32[]{:S(2)}, u32[]{:S(2)}) async-start(bf16[16,512,128]{2,1,0:T(8,128)(2,1)} %shard_map.134), calls=%async_computation.2 | async-start | bytes 4194304 | tf_op jit(solution)/shard_map/all_to_all | solution.py:491
  86.3 3.9 %collective-permute-start.4 = (f32[12,384]{1,0:T(8,128)S(1)}, f32[12,384]{1,0:T(8,128)S(1)}, u32[]{:S(2)}, u32[]{:S(2)}) collective-permute-start(f32[12,384]{1,0:T(8,128)S(1)} %add_select_fusion.3), channel_id=1, source_target_pairs={{0,2},{2,0},{4,6},{6,4},{8,10},{10,8},{12,14},{14,12},{16,18},{18,... | collective-permute-start | bytes 55304 | tf_op jit(solution)/shard_map/ppermute | solution.py:485
  90.2 4.0 %collective-permute-start.5 = (f32[24,384]{1,0:T(8,128)S(1)}, f32[24,384]{1,0:T(8,128)S(1)}, u32[]{:S(2)}, u32[]{:S(2)}) collective-permute-start(f32[24,384]{1,0:T(8,128)S(1)} %pad_maximum_fusion.1), channel_id=1, source_target_pairs={{0,4},{2,6},{4,0},{6,2},{8,12},{10,14},{12,8},{14,10},{16,20},{18,... | collective-permute-start | bytes 110600 | tf_op jit(solution)/shard_map/ppermute | solution.py:485
